TPU v7x, 128 devices: a whole 4x4x4 slice. The times are simulated.
128 devices in a mesh: expert: 32 (over y, z, core), shard: 4 (over x).
Axes of the slice: x: 4, y: 4, z: 4, core: 2. Of those that a mesh axis runs over, the one named last changes fastest.
Arguments:
- tokens: bfloat16 [32768, 2880], P('expert', 'shard'), may hold values from -6 to 6
- gate_weight: bfloat16 [64, 2880, 1536], P(None, 'expert', 'shard'), may hold values from -0.109375 to 0.109375
- up_weight: bfloat16 [64, 2880, 1536], P(None, 'expert', 'shard'), may hold values from -0.109375 to 0.109375
- down_weight: bfloat16 [64, 2880, 1536], P(None, 'expert', 'shard'), may hold values from -0.15625 to 0.15625
- block_counts: int32 [64], P('expert'), may hold values from 0 to 8, as said below
- block_tokens: int32 [256, 256], P('expert'), may hold values from 0 to 1023, as said below
Outputs:
- expert_out: bfloat16 [65536, 2880], P(('expert', 'shard'))
Inputs may be any that keep to these rules, and one draw needn't show every extreme that they name: `block_counts`: for each section, the counts of its 2 experts sum to at most 8; some section is full in every draw. `block_tokens`: rows of the section's own dispatched tokens; every row of a section appears in exactly two positions of its slots.
All inputs are finite; a program needn't handle non-finite values.
Results may differ from a plain program's by a relative error of at most 0.015.
Values may be sent and summed in bfloat16 or wider, within the bound.
A program may use at most 256 MiB of HBM per device.

v0:
```python
import jax
import jax.numpy as jnp
from jax import lax
from jax.sharding import PartitionSpec as P

GROUP = 32


def shared_scale(amax):
    result = jnp.full(amax.shape, 2.0 ** (-32), jnp.float32)
    for exponent in range(-29, 9):
        result = jnp.where(amax >= 2.0**exponent, jnp.float32(2.0 ** (exponent - 2)), result)
    return result


def nearest_code(ratio):
    magnitude = jnp.abs(ratio)
    level = 0.5 * (magnitude > 0.25).astype(jnp.float32)
    level = level + 0.5 * (magnitude >= 0.75).astype(jnp.float32)
    level = level + 0.5 * (magnitude > 1.25).astype(jnp.float32)
    level = level + 0.5 * (magnitude >= 1.75).astype(jnp.float32)
    level = level + (magnitude > 2.5).astype(jnp.float32)
    level = level + (magnitude >= 3.5).astype(jnp.float32)
    level = level + 2.0 * (magnitude > 5.0).astype(jnp.float32)
    return jnp.sign(ratio) * level


def encode(weight):
    count, rows, cols = weight.shape
    grouped = weight.astype(jnp.float32).reshape(count, rows, cols // GROUP, GROUP)
    amax = jnp.max(jnp.abs(grouped), axis=-1)
    scales = shared_scale(amax).astype(jnp.bfloat16)
    coded = nearest_code(grouped / scales.astype(jnp.float32)[..., None]).astype(jnp.bfloat16)
    return (coded, scales)


def decode(coded, scales):
    restored = (coded.astype(jnp.float32) * scales.astype(jnp.float32)[..., None]).astype(
        jnp.bfloat16
    )
    return restored.reshape(coded.shape[0], coded.shape[1], -1)


def activate(gate, up):
    return (up + 1.0) * gate * jax.nn.sigmoid(1.702 * gate)


def body(tokens, gate_weight, up_weight, down_weight, block_counts, block_tokens):
    slots = block_tokens.shape[0]
    block = block_tokens.shape[1]
    shards = lax.axis_size("shard")
    ends = jnp.cumsum(block_counts)

    def slot_local(index):
        return jnp.sum((index >= ends[:-1]).astype(jnp.int32))

    coded_gate, scale_gate = encode(gate_weight)
    coded_up, scale_up = encode(up_weight)
    coded_down, scale_down = encode(down_weight)
    features = lax.all_gather(tokens, "shard", axis=1, tiled=True)
    got_gate, got_up, got_down, got_sg, got_su, got_sd = (
        lax.all_to_all(coded_gate, "expert", split_axis=0, concat_axis=1, tiled=True),
        lax.all_to_all(coded_up, "expert", split_axis=0, concat_axis=1, tiled=True),
        lax.all_to_all(coded_down, "expert", split_axis=0, concat_axis=1, tiled=True),
        lax.all_to_all(scale_gate, "expert", split_axis=0, concat_axis=1, tiled=True),
        lax.all_to_all(scale_up, "expert", split_axis=0, concat_axis=1, tiled=True),
        lax.all_to_all(scale_down, "expert", split_axis=0, concat_axis=1, tiled=True),
    )
    w_gate = decode(got_gate, got_sg)
    w_up = decode(got_up, got_su)
    cols = w_gate.shape[2]

    def slot(index):
        local = slot_local(index)

        def slot_work(position):
            picked = jnp.take(features, block_tokens[position], axis=0)
            gate = jnp.dot(picked, w_gate[local], preferred_element_type=jnp.float32)
            up = jnp.dot(picked, w_up[local], preferred_element_type=jnp.float32)
            return activate(gate, up).astype(jnp.bfloat16)

        def slot_skip(position):
            return jnp.zeros((block, cols), jnp.bfloat16)

        return lax.cond(index < ends[-1], slot_work, slot_skip, index)

    hidden = lax.map(slot, jnp.arange(slots, dtype=jnp.int32))
    w_down = decode(got_down, got_sd)
    width = w_down.shape[1]

    def project(rows_hidden, index):
        local = slot_local(index)

        def project_work(position):
            return lax.dot_general(
                rows_hidden,
                w_down[local],
                (((1,), (1,)), ((), ())),
                preferred_element_type=jnp.float32,
            )

        def project_skip(position):
            return jnp.zeros((rows_hidden.shape[0], width), jnp.float32)

        return lax.cond(index < ends[-1], project_work, project_skip, index)

    own_rows = slots * block // shards
    indices = jnp.arange(lax.axis_size("shard") * own_rows // block, dtype=jnp.int32)
    made = lax.map(lambda index: project(hidden[index], index), indices)
    return lax.psum_scatter(
        made.reshape(lax.axis_size("shard") * own_rows, width).astype(jnp.bfloat16),
        "shard",
        scatter_dimension=0,
        tiled=True,
    )


def solution(mesh):
    in_specs = (
        P("expert", "shard"),
        P(None, "expert", "shard"),
        P(None, "expert", "shard"),
        P(None, "expert", "shard"),
        P("expert"),
        P("expert", None),
    )
    out_specs = P(("expert", "shard"), None)
    return jax.shard_map(body, mesh=mesh, in_specs=in_specs, out_specs=out_specs, check_vma=False)
```

profile of v0, /device:TPU:1, one launch (start us, length us, event | category | flops | bytes accessed | tf_op | source)
XLA Modules:
  0.0 826.1 jit_solution(1166986971018296275)
XLA Ops:
  6.5 8.4 %copy.46 = bf16[64,90,384]{1,2,0:T(8,128)(2,1)} copy(bf16[64,90,384]{2,0,1:T(8,128)(2,1)} %param.16) | data formatting | bytes 8847360 | tf_op args[2]
  22.8 9.9 %all-to-all-start.1 = ((bf16[64,90,12]{1,2,0:T(8,128)(2,1)}), bf16[64,90,12]{1,2,0:T(8,128)(2,1)S(1)}, u32[]{:S(2)}, u32[]{:S(2)}) async-start(bf16[64,90,12]{1,2,0:T(8,128)(2,1)} %get-tuple-element.223), calls=%async_computation.1 | async-start | bytes 524288 | tf_op jit(solution)/shard_map/all_to_all | solution.py:66
  32.7 8.3 %copy.51 = bf16[64,90,384]{1,2,0:T(8,128)(2,1)} copy(bf16[64,90,384]{2,0,1:T(8,128)(2,1)} %param.15) | data formatting | bytes 8847360 | tf_op args[1]
  83.8 16.2 %multiply_convert_fusion.2 = bf16[64,90,12,32]{1,3,2,0:T(8,128)(2,1)} fusion(bf16[64,90,12,32]{1,3,2,0:T(8,128)(2,1)} %bitcast.124, f32[64,90,12]{1,2,0:T(8,128)S(1)} %get-tuple-element.222), kind=kLoop, calls=%fused_computation.44 | loop fusion | flops 57507840 | bytes 9123840 | tf_op jit(solution)/shard_map/convert_element_type | solution.py:33
  107.6 16.1 %multiply_convert_fusion.1 = bf16[64,90,12,32]{1,3,2,0:T(8,128)(2,1)} fusion(bf16[64,90,12,32]{1,3,2,0:T(8,128)(2,1)} %bitcast.122, f32[64,90,12]{1,2,0:T(8,128)S(1)} %get-tuple-element.220), kind=kLoop, calls=%fused_computation.43 | loop fusion | flops 57507840 | bytes 9123840 | tf_op jit(solution)/shard_map/convert_element_type | solution.py:33
  123.7 61.8 %all-to-all-done = bf16[64,90,12,32]{1,3,2,0:T(8,128)(2,1)} async-done(((bf16[64,90,12,32]{1,3,2,0:T(8,128)(2,1)}), bf16[64,90,12,32]{1,3,2,0:T(8,128)(2,1)}, u32[]{:S(2)}, u32[]{:S(2)}) %all-to-all-start) | async-done | bytes 4423712 | tf_op jit(solution)/shard_map/all_to_all | solution.py:63
  185.6 14.6 %all-to-all-start.2 = ((bf16[64,90,12,32]{1,3,2,0:T(8,128)(2,1)}), bf16[64,90,12,32]{1,3,2,0:T(8,128)(2,1)}, u32[]{:S(2)}, u32[]{:S(2)}) async-start(bf16[64,90,12,32]{1,3,2,0:T(8,128)(2,1)} %multiply_convert_fusion.1), calls=%async_computation.2 | async-start | bytes 12582912 | tf_op jit(solution)/shard_map/all_to_all | solution.py:62
  200.9 16.1 %multiply_convert_fusion = bf16[64,90,12,32]{1,3,2,0:T(8,128)(2,1)} fusion(bf16[64,90,12,32]{1,3,2,0:T(8,128)(2,1)} %bitcast.120, f32[64,90,12]{1,2,0:T(8,128)S(1)} %get-tuple-element.218), kind=kLoop, calls=%fused_computation.42 | loop fusion | flops 57507840 | bytes 9123840 | tf_op jit(solution)/shard_map/convert_element_type | solution.py:33
  217.0 61.1 %all-to-all-done.2 = bf16[64,90,12,32]{1,3,2,0:T(8,128)(2,1)} async-done(((bf16[64,90,12,32]{1,3,2,0:T(8,128)(2,1)}), bf16[64,90,12,32]{1,3,2,0:T(8,128)(2,1)}, u32[]{:S(2)}, u32[]{:S(2)}) %all-to-all-start.2) | async-done | bytes 4423712 | tf_op jit(solution)/shard_map/all_to_all | solution.py:62
  278.1 14.6 %all-to-all-start.4 = ((bf16[64,90,12,32]{1,3,2,0:T(8,128)(2,1)}), bf16[64,90,12,32]{1,3,2,0:T(8,128)(2,1)}, u32[]{:S(2)}, u32[]{:S(2)}) async-start(bf16[64,90,12,32]{1,3,2,0:T(8,128)(2,1)} %multiply_convert_fusion), calls=%async_computation.4 | async-start | bytes 12582912 | tf_op jit(solution)/shard_map/all_to_all | solution.py:64
  294.4 9.1 %convert_bitcast_fusion.2 = f32[2,32,90,12,32]{2,4,3,0,1:T(8,128)} fusion(bf16[32,2,90,12,32]{2,4,3,1,0:T(8,128)(2,1)} %bitcast.38), kind=kLoop, calls=%fused_computation.41 | loop fusion | flops 2211840 | bytes 13271040 | tf_op jit(solution)/shard_map/convert_element_type | solution.py:38
  303.5 20.3 %copy.47 = f32[2,32,90,12,32]{2,1,4,3,0:T(8,128)} copy(f32[2,32,90,12,32]{2,4,3,0,1:T(8,128)} %convert_bitcast_fusion.2) | data formatting | bytes 17694720 | tf_op jit(solution)/shard_map/convert_element_type | solution.py:38
  323.8 13.8 %reshape.383 = f32[2,2880,384]{1,2,0:T(8,128)} reshape(f32[2,32,90,12,32]{2,1,4,3,0:T(8,128)} %copy.47) | data formatting | bytes 17694720 | tf_op jit(solution)/shard_map/convert_element_type | solution.py:38
  350.6 9.1 %convert_bitcast_fusion.1 = f32[2,32,90,12,32]{2,4,3,0,1:T(8,128)} fusion(bf16[32,2,90,12,32]{2,4,3,1,0:T(8,128)(2,1)} %bitcast.40), kind=kLoop, calls=%fused_computation.40 | loop fusion | flops 2211840 | bytes 13271040 | tf_op jit(solution)/shard_map/convert_element_type | solution.py:38
  359.7 20.0 %copy.52 = f32[2,32,90,12,32]{2,1,4,3,0:T(8,128)} copy(f32[2,32,90,12,32]{2,4,3,0,1:T(8,128)} %convert_bitcast_fusion.1) | data formatting | bytes 17694720 | tf_op jit(solution)/shard_map/convert_element_type | solution.py:38
  379.7 13.8 %reshape.387 = f32[2,2880,384]{1,2,0:T(8,128)} reshape(f32[2,32,90,12,32]{2,1,4,3,0:T(8,128)} %copy.52) | data formatting | bytes 17694720 | tf_op jit(solution)/shard_map/convert_element_type | solution.py:38
  406.4 9.1 %convert_bitcast_fusion = f32[2,32,90,12,32]{2,4,3,0,1:T(8,128)} fusion(bf16[32,2,90,12,32]{2,4,3,1,0:T(8,128)(2,1)} %bitcast.42), kind=kLoop, calls=%fused_computation.39 | loop fusion | flops 2211840 | bytes 13271040 | tf_op jit(solution)/shard_map/convert_element_type | solution.py:38
  415.5 20.1 %copy.60 = f32[2,32,90,12,32]{2,1,4,3,0:T(8,128)} copy(f32[2,32,90,12,32]{2,4,3,0,1:T(8,128)} %convert_bitcast_fusion) | data formatting | bytes 17694720 | tf_op jit(solution)/shard_map/convert_element_type | solution.py:38
  435.6 13.8 %reshape.391 = f32[2,2880,384]{1,2,0:T(8,128)} reshape(f32[2,32,90,12,32]{2,1,4,3,0:T(8,128)} %copy.60) | data formatting | bytes 17694720 | tf_op jit(solution)/shard_map/convert_element_type | solution.py:38
  462.4 8.5 %copy.56 = bf16[1024,2880]{1,0:T(8,128)(2,1)} copy(bf16[1024,2880]{0,1:T(8,128)(2,1)} %all-gather.2.cloned.1.call-done) | data formatting | bytes 11796480 | tf_op jit(solution)/shard_map/while | solution.py:87
  470.9 152.8 %while.20 = (s32[]{:T(128)}, bf16[8,256,384]{2,1,0:T(8,128)(2,1)}, s32[8]{0:T(128)S(1)}, s32[2]{0:T(128)S(1)}, s32[8,256]{1,0:T(8,128)}, /*index=5*/bf16[1024,28...) while((s32[]{:T(128)}, bf16[8,256,384]{2,1,0:T(8,128)(2,1)}, ...), condition=%wide.region_6.7_spmd, body=%wide.region_3.6_spmd.sunk | while | flops 1134726400 | bytes 11709981 | solution.py:87
  474.7 14.6 %conditional.4 = (bf16[1,256,384]{2,1,0:T(8,128)(2,1)S(1)}) conditional(s32[]{:T(128)} %convert_element_type.298, () %tuple.68, (s32[]{:T(128)}, s32[8,256]{1,0:T(8,128)}, bf16[1024,2880]{1,0:T(8,128)(2,1)}, s32[1]{0:T(128)}, bf16[2,2880,384]{2,1,0:T(8,128)(2,1)}, /*index=5*/bf16[2,2880,384]{2,1,0:T(8,128)(2,1)}) %tuple.69), branch_computations={%region_4.4_spmd, %region_5.5_spmd} | conditional | flops 1134726400 | bytes 11316056 | solution.py:85
  493.8 14.6 %conditional.4 = (bf16[1,256,384]{2,1,0:T(8,128)(2,1)S(1)}) conditional(s32[]{:T(128)} %convert_element_type.298, () %tuple.68, (s32[]{:T(128)}, s32[8,256]{1,0:T(8,128)}, bf16[1024,2880]{1,0:T(8,128)(2,1)}, s32[1]{0:T(128)}, bf16[2,2880,384]{2,1,0:T(8,128)(2,1)}, /*index=5*/bf16[2,2880,384]{2,1,0:T(8,128)(2,1)}) %tuple.69), branch_computations={%region_4.4_spmd, %region_5.5_spmd} | conditional | flops 1134726400 | bytes 11316056 | solution.py:85
  512.9 14.6 %conditional.4 = (bf16[1,256,384]{2,1,0:T(8,128)(2,1)S(1)}) conditional(s32[]{:T(128)} %convert_element_type.298, () %tuple.68, (s32[]{:T(128)}, s32[8,256]{1,0:T(8,128)}, bf16[1024,2880]{1,0:T(8,128)(2,1)}, s32[1]{0:T(128)}, bf16[2,2880,384]{2,1,0:T(8,128)(2,1)}, /*index=5*/bf16[2,2880,384]{2,1,0:T(8,128)(2,1)}) %tuple.69), branch_computations={%region_4.4_spmd, %region_5.5_spmd} | conditional | flops 1134726400 | bytes 11316056 | solution.py:85
  532.0 14.6 %conditional.4 = (bf16[1,256,384]{2,1,0:T(8,128)(2,1)S(1)}) conditional(s32[]{:T(128)} %convert_element_type.298, () %tuple.68, (s32[]{:T(128)}, s32[8,256]{1,0:T(8,128)}, bf16[1024,2880]{1,0:T(8,128)(2,1)}, s32[1]{0:T(128)}, bf16[2,2880,384]{2,1,0:T(8,128)(2,1)}, /*index=5*/bf16[2,2880,384]{2,1,0:T(8,128)(2,1)}) %tuple.69), branch_computations={%region_4.4_spmd, %region_5.5_spmd} | conditional | flops 1134726400 | bytes 11316056 | solution.py:85
  551.1 14.6 %conditional.4 = (bf16[1,256,384]{2,1,0:T(8,128)(2,1)S(1)}) conditional(s32[]{:T(128)} %convert_element_type.298, () %tuple.68, (s32[]{:T(128)}, s32[8,256]{1,0:T(8,128)}, bf16[1024,2880]{1,0:T(8,128)(2,1)}, s32[1]{0:T(128)}, bf16[2,2880,384]{2,1,0:T(8,128)(2,1)}, /*index=5*/bf16[2,2880,384]{2,1,0:T(8,128)(2,1)}) %tuple.69), branch_computations={%region_4.4_spmd, %region_5.5_spmd} | conditional | flops 1134726400 | bytes 11316056 | solution.py:85
  570.2 14.6 %conditional.4 = (bf16[1,256,384]{2,1,0:T(8,128)(2,1)S(1)}) conditional(s32[]{:T(128)} %convert_element_type.298, () %tuple.68, (s32[]{:T(128)}, s32[8,256]{1,0:T(8,128)}, bf16[1024,2880]{1,0:T(8,128)(2,1)}, s32[1]{0:T(128)}, bf16[2,2880,384]{2,1,0:T(8,128)(2,1)}, /*index=5*/bf16[2,2880,384]{2,1,0:T(8,128)(2,1)}) %tuple.69), branch_computations={%region_4.4_spmd, %region_5.5_spmd} | conditional | flops 1134726400 | bytes 11316056 | solution.py:85
  589.3 14.6 %conditional.4 = (bf16[1,256,384]{2,1,0:T(8,128)(2,1)S(1)}) conditional(s32[]{:T(128)} %convert_element_type.298, () %tuple.68, (s32[]{:T(128)}, s32[8,256]{1,0:T(8,128)}, bf16[1024,2880]{1,0:T(8,128)(2,1)}, s32[1]{0:T(128)}, bf16[2,2880,384]{2,1,0:T(8,128)(2,1)}, /*index=5*/bf16[2,2880,384]{2,1,0:T(8,128)(2,1)}) %tuple.69), branch_computations={%region_4.4_spmd, %region_5.5_spmd} | conditional | flops 1134726400 | bytes 11316056 | solution.py:85
  608.4 14.6 %conditional.4 = (bf16[1,256,384]{2,1,0:T(8,128)(2,1)S(1)}) conditional(s32[]{:T(128)} %convert_element_type.298, () %tuple.68, (s32[]{:T(128)}, s32[8,256]{1,0:T(8,128)}, bf16[1024,2880]{1,0:T(8,128)(2,1)}, s32[1]{0:T(128)}, bf16[2,2880,384]{2,1,0:T(8,128)(2,1)}, /*index=5*/bf16[2,2880,384]{2,1,0:T(8,128)(2,1)}) %tuple.69), branch_computations={%region_4.4_spmd, %region_5.5_spmd} | conditional | flops 1134726400 | bytes 11316056 | solution.py:85
  623.7 77.2 %while.21 = (s32[]{:T(128)}, bf16[8,256,2880]{1,2,0:T(8,128)(2,1)}, s32[8]{0:T(128)S(1)}, s32[2]{0:T(128)S(1)}, bf16[8,256,384]{2,1,0:T(8,128)(2,1)}, /*index=5*/bf16[2,2880,384]{2,1,0:T(8,128)(2,1)}, s32[]{:T(128)}) while((s32[]{:T(128)}, bf16[8,256,2880]{1,2,0:T(8,128)(2,1)}, s32[8]{0:T(128)S(1)}, s32[2]{0:T(128)S(1)}, ...), condition=%wide.region_11.12_spmd, body=%wide.region_8.11_spmd.sunk | while | flops 566231040 | bytes 6832889 | solution.py:109
  700.9 10.4 %copy.72 = bf16[8,360,8,256]{3,2,0,1:T(8,128)(2,1)} copy(bf16[8,360,8,256]{3,2,1,0:T(8,128)(2,1)} %bitcast.126) | data formatting | bytes 23592960 | tf_op jit(solution)/shard_map/convert_element_type | solution.py:111
  711.3 107.8 %reduce-scatter.2.cloned.1.call-done = bf16[512,2880]{0,1:T(8,128)(2,1)} async-done(((bf16[2048,2880]{0,1:T(8,128)(2,1)}), bf16[512,2880]{0,1:T(8,128)(2,1)}) %reduce-scatter.2.cloned.1.call-update) | async-done | bytes 2949136 | tf_op jit(solution)/shard_map/reduce_scatter | solution.py:110
  (153 shorter events, 295.1 us)
Async XLA Ops:
  22.8 40.4 %all-to-all-start.1 = ((bf16[64,90,12]{1,2,0:T(8,128)(2,1)}), bf16[64,90,12]{1,2,0:T(8,128)(2,1)S(1)}, u32[]{:S(2)}, u32[]{:S(2)}) async-start(bf16[64,90,12]{1,2,0:T(8,128)(2,1)} %get-tuple-element.223), calls=%async_computation.1 | async-start | bytes 524288 | tf_op jit(solution)/shard_map/all_to_all | solution.py:66
  63.2 16.4 %all-to-all-start.3 = ((bf16[64,90,12]{1,2,0:T(8,128)(2,1)}), bf16[64,90,12]{1,2,0:T(8,128)(2,1)S(1)}, u32[]{:S(2)}, u32[]{:S(2)}) async-start(bf16[64,90,12]{1,2,0:T(8,128)(2,1)} %get-tuple-element.221), calls=%async_computation.3 | async-start | bytes 524288 | tf_op jit(solution)/shard_map/all_to_all | solution.py:65
  79.6 20.4 %all-to-all-start.5 = ((bf16[64,90,12]{1,2,0:T(8,128)(2,1)}), bf16[64,90,12]{1,2,0:T(8,128)(2,1)S(1)}, u32[]{:S(2)}, u32[]{:S(2)}) async-start(bf16[64,90,12]{1,2,0:T(8,128)(2,1)} %get-tuple-element.219), calls=%async_computation.5 | async-start | bytes 524288 | tf_op jit(solution)/shard_map/all_to_all | solution.py:67
  100.1 85.5 %all-to-all-start = ((bf16[64,90,12,32]{1,3,2,0:T(8,128)(2,1)}), bf16[64,90,12,32]{1,3,2,0:T(8,128)(2,1)}, u32[]{:S(2)}, u32[]{:S(2)}) async-start(bf16[64,90,12,32]{1,3,2,0:T(8,128)(2,1)} %multiply_convert_fusion.2), calls=%async_computation | async-start | bytes 12582912 | tf_op jit(solution)/shard_map/all_to_all | solution.py:63
  185.6 92.6 %all-to-all-start.2 = ((bf16[64,90,12,32]{1,3,2,0:T(8,128)(2,1)}), bf16[64,90,12,32]{1,3,2,0:T(8,128)(2,1)}, u32[]{:S(2)}, u32[]{:S(2)}) async-start(bf16[64,90,12,32]{1,3,2,0:T(8,128)(2,1)} %multiply_convert_fusion.1), calls=%async_computation.2 | async-start | bytes 12582912 | tf_op jit(solution)/shard_map/all_to_all | solution.py:62
  200.2 262.2 %all-gather.2.cloned.1.call-start = ((), (), s32[]{:S(2)}) async-start(), calls=%async_computation.7 | async-start | bytes 7372800 | tf_op jit(solution)/shard_map/all_gather | solution.py:60
  217.0 75.9 %copy-start = (s32[2]{0:T(128)S(1)}, s32[2]{0:T(128)}, u32[]{:S(2)}) copy-start(s32[2]{0:T(128)} %param.18) | copy-start | bytes 28
  278.1 128.3 %all-to-all-start.4 = ((bf16[64,90,12,32]{1,3,2,0:T(8,128)(2,1)}), bf16[64,90,12,32]{1,3,2,0:T(8,128)(2,1)}, u32[]{:S(2)}, u32[]{:S(2)}) async-start(bf16[64,90,12,32]{1,3,2,0:T(8,128)(2,1)} %multiply_convert_fusion), calls=%async_computation.4 | async-start | bytes 12582912 | tf_op jit(solution)/shard_map/all_to_all | solution.py:64
  292.7 526.3 %reduce-scatter.2.cloned.1.call-start = ((), (), s32[]{:S(2)}) async-start(), calls=%async_computation.8 | async-start | bytes 14745600 | tf_op jit(solution)/shard_map/reduce_scatter | solution.py:110
Sparse Core Ops, SparseCore 0:
  202.7 63.3 all-gather.1
  711.4 107.5 reduce-scatter.1
where the time goes:
time: 836 us; the launch traced here: 826 us
  local copies, waits for them, and re-layouts  255 us (31%)
  waiting for transfers between devices  238 us (28%)
  other arithmetic  125 us (15%)
  loops' own time  71.4 us (9%)
  matrix products  64.3 us (8%)
  starting transfers between devices  58.5 us (7%)
  between operations  13.8 us (2%)
    reduce_scatter x1, waiting for transfers between devices, body(): lax.psum_scatter(made.reshape(lax.axis_size('shard') * own_rows, width).a...  108 us
    convert_element_type x6, local copies, waits for them, and re-layouts, decode(): coded.astype(jnp.float32) * scales.astype(jnp.float32)[..., None]  102 us
    all_to_all x1, waiting for transfers between devices, body(): lax.all_to_all(coded_up, 'expert', split_axis=0, concat_axis=1, tiled=True)  61.8 us
    all_to_all x1, waiting for transfers between devices, body(): lax.all_to_all(coded_gate, 'expert', split_axis=0, concat_axis=1, tiled=T...  61.1 us
    gather x8, local copies, waits for them, and re-layouts, slot_work(): picked = jnp.take(features, block_tokens[position], axis=0)  52.9 us
    convert_element_type x3, other arithmetic, encode(): nearest_code(grouped / scales.astype(jnp.float32)[..., None])  48.4 us
    convert_element_type x3, other arithmetic, decode(): coded.astype(jnp.float32) * scales.astype(jnp.float32)[..., None]  27.3 us
    unnamed x8, local copies, waits for them, and re-layouts  25.1 us
  transfers between devices with their start and end apart: 8, of which 4 were waited for; matrix products, arithmetic and copies ran while one was open for 30% of the time, Pallas kernels for 0%

commit v1 on v0

v1 whole, which is shorter than its diff:
```python
import functools

import jax
import jax.numpy as jnp
import numpy as np
from jax import lax
from jax.experimental import pallas as pl
from jax.experimental.pallas import tpu as pltpu
from jax.sharding import PartitionSpec as P

GROUP = 32
LANES = 128
BF16 = jnp.bfloat16
F32 = jnp.float32
MESH = pl.DeviceIdType.MESH

RING = 4
D = 2880
ROWS = 90
PAD = 96
FEAT = 720
WIDE = 8 * PAD
COLS = 384
TOK = 1024
BLOCK = 256
SLOTS = 8
TILE = 16
CHUNKS = 3
OUTB = 384


def place_matrix():
    m = np.zeros((FEAT, WIDE), np.float32)
    for k in range(FEAT):
        m[k, k // ROWS * PAD + k % ROWS] = 1
    return m


def group_matrix():
    lane = np.arange(LANES) // GROUP
    return (lane[:, None] == lane[None, :]).astype(np.float32)


def order_matrix():
    m = np.zeros((9, 12 * LANES, OUTB), np.float32)
    for d in range(D):
        pair, rest = divmod(d, 2 * ROWS)
        core, row = divmod(rest, ROWS)
        part, row = divmod(row, 48)
        chunk, row = divmod(row, TILE)
        half, pair = divmod(pair, 8)
        block, col = divmod(d, OUTB)
        if block == 3 and half == 1:
            block = 8
        m[block, ((2 * core + part) * CHUNKS + chunk) * LANES + pair * TILE + row, col] = 1
    return m


def power_floor(value):
    far = value * 8388609.0
    return far - (far - value)


def restore(weight, groups):
    power = power_floor(jnp.abs(weight) * 0.751953125)
    square = power * power
    sixth = (square * square) * (square * 2.0**60)
    total = jnp.dot(sixth.astype(BF16), groups, preferred_element_type=F32)
    top = power_floor(jnp.exp2((jnp.log2(total) - 60.0) * (1.0 / 6.0)) * 0.8)
    top = jnp.minimum(jnp.maximum(top, 2.0**-30), 2.0**8)
    magic = jnp.maximum(power, top * 0.25) * (1.5 * 2.0**22)
    rounded = (weight + magic) - magic
    limit = top * 1.5
    return jnp.minimum(jnp.maximum(rounded, -limit), limit).astype(BF16)


def kernel(
    tokens, gate_w, up_w, down_w, sel, expert, place, groups, order,
    out, mid, xs, midd,
    ob, inbox, tok, stage, in_0, in_1, in_2, hid2, hid, ob_out, fin,
    stage_sem, order_sem, s1_send, s1_recv, s2_send, s2_recv, xs_send, xs_recv,
    d1_send, d1_recv, d2_send, d2_recv, tok_send, tok_recv, hid_send, hid_recv, out_send, out_recv,
):
    in_d = (in_0, in_1, in_2)
    me, x = lax.axis_index("expert"), lax.axis_index("shard")
    y, z, c = me // 8, (me // 2) % 4, me % 2

    def device(yy, zz, cc, xx):
        return ((yy * 4 + zz) * 2 + cc, xx)

    def ring(at, step):
        return (at + step) % RING

    def remote(src, dst, send, recv, target):
        return pltpu.make_async_remote_copy(
            src_ref=src, dst_ref=dst, send_sem=send, recv_sem=recv, device_id=target, device_id_type=MESH
        )

    def landed(ref, sem):
        pltpu.make_async_copy(ref, ref, sem).wait()

    barrier = pltpu.get_barrier_semaphore()
    peers = [device(y, z, 1 - c, x)]
    for step in (1, 2, 3):
        for cc in (c, 1 - c):
            peers += [device(ring(y, step), z, cc, x), device(y, ring(z, step), cc, x), device(y, z, cc, ring(x, step))]
    for peer in peers:
        pl.semaphore_signal(barrier, inc=1, device_id=peer, device_id_type=MESH)

    def load(n, slot):
        q, step = n // 4, (n + 1) % 4
        return [
            pltpu.make_async_copy(gate_w.at[ring(y, step), :, :, q], stage.at[slot, 0], stage_sem.at[slot, 0]),
            pltpu.make_async_copy(up_w.at[:, ring(z, step), :, q], stage.at[slot, 1], stage_sem.at[slot, 1]),
        ]

    def load_down(n, slot):
        return [
            pltpu.make_async_copy(down_w.at[n, :, :, e], stage.at[slot, e], stage_sem.at[slot, e]) for e in (0, 1)
        ]

    for copy in load(0, 0):
        copy.start()

    @pl.loop(0, 128)
    def _(n):
        ob[n // 64, n % 64, 80:PAD, :] = jnp.zeros((16, COLS), BF16)

    @pl.loop(0, 4)
    def _(n):
        rows = pl.ds(n * 256, 256)
        tok[x, rows, :] = jnp.dot(tokens[rows, :], place[...], preferred_element_type=F32).astype(BF16)

    pl.semaphore_wait(barrier, len(peers))

    right, left = device(y, z, c, ring(x, 1)), device(y, z, c, ring(x, 3))
    tok_near = [
        remote(tok.at[x], tok.at[x], tok_send.at[0], tok_recv.at[0], right),
        remote(tok.at[x], tok.at[x], tok_send.at[1], tok_recv.at[1], left),
    ]
    for copy in tok_near:
        copy.start()
    lower, upper = pl.ds(0, 512), pl.ds(512, 512)
    tok_far = [
        remote(tok.at[ring(x, 3), lower], tok.at[ring(x, 3), lower], tok_send.at[2], tok_recv.at[2], right),
        remote(tok.at[ring(x, 1), upper], tok.at[ring(x, 1), upper], tok_send.at[3], tok_recv.at[3], left),
    ]

    def encode(slot, i, dst):
        half, zc = i // 8, i % 8
        for lane in range(COLS // LANES):
            cols = slice(lane * LANES, (lane + 1) * LANES)
            weight = stage[slot, half, zc // 2, zc % 2, :, cols].astype(F32)
            ob[dst[0], dst[1], 0:ROWS, cols] = restore(weight, groups[...])

    def first(ab, q, step):
        to = ring(y, step) if ab == 0 else ring(z, step)
        target = device(to, z, c, x) if ab == 0 else device(y, to, c, x)
        here = y if ab == 0 else z
        src, dst = ob.at[q, pl.ds(32 * ab + to * 8, 8)], mid.at[ab, q, here]
        return src, dst, s1_send.at[ab, q, step], s1_recv.at[ab, q, step], target

    @pl.loop(0, 8)
    def _(n):
        slot, q, step = n % 2, n // 4, (n + 1) % 4
        for copy in load(n, slot):
            copy.wait()

        @pl.when(n < 7)
        def _():
            for copy in load(n + 1, 1 - slot):
                copy.start()

        @pl.loop(0, 16, unroll=4)
        def _(i):
            half = i // 8
            to = (1 - half) * ring(y, step) + half * (4 + ring(z, step))
            encode(slot, i, (q, to * 8 + i % 8))

        @pl.when(step == 0)
        def _():
            for ab in (0, 1):
                src, dst, _, recv, _ = first(ab, q, 0)
                pltpu.make_async_copy(src, dst, recv).start()

        @pl.when(step != 0)
        def _():
            for ab in (0, 1):
                remote(*first(ab, q, step)).start()

    for copy in load_down(0, 0):
        copy.start()

    def second(q):
        local, far = [], []
        for step in (2, 1, 3, 0):
            for dc in (0, 1):
                cc = (c + dc) % 2
                zz, yy = ring(z, step), ring(y, step)
                a = (mid.at[0, q, :, zz * 2 + cc], inbox.at[pl.ds(q * 8, 4), z, c])
                b = (mid.at[1, q, :, yy * 2 + cc], inbox.at[q * 8 + 4 + y, :, c])
                if step == 0 and dc == 0:
                    local += [pltpu.make_async_copy(*pair, s2_recv.at[ab, q, 0, 0]) for ab, pair in enumerate((a, b))]
                    continue
                for ab, pair, target in ((0, a, device(y, zz, cc, x)), (1, b, device(yy, z, cc, x))):
                    far.append(remote(*pair, s2_send.at[ab, q, step, dc], s2_recv.at[ab, q, step, dc], target))
        return local, far

    def pass_on(q):
        for ab in (0, 1):
            for step in range(RING):
                _, dst, _, recv, _ = first(ab, q, step)
                landed(dst, recv)
        local, far = second(q)
        for copy in far + local:
            copy.start()
        return local, far

    def sent(q):
        for ab in (0, 1):
            for step in (1, 2, 3):
                remote(*first(ab, q, step)).wait_send()

    second_0 = pass_on(0)
    for near, far in zip(tok_near, tok_far):
        near.wait_recv()
        far.start()

    sent(0)

    @pl.loop(0, 4)
    def _(n):
        slot = n % 2
        for copy in load_down(n, slot):
            copy.wait()

        @pl.when(n < 3)
        def _():
            for copy in load_down(n + 1, 1 - slot):
                copy.start()

        @pl.loop(0, 16, unroll=4)
        def _(i):
            e, zz, cc = i // 8, (i // 2) % 4, i % 2
            encode(slot, i, (0, cc * 32 + (1 - e) * (n * 4 + zz) + e * (16 + zz * 4 + n)))

    shuffles = []
    for cc in (0, 1):
        for h in (0, 1):
            to = 2 * c + h
            src, dst = ob.at[0, pl.ds(cc * 32, 32), pl.ds(48 * h, 48)], xs.at[x]
            own = jnp.logical_and(cc == c, to == x)
            far = remote(src, dst, xs_send.at[cc, h], xs_recv.at[x], device(y, z, cc, to))
            near = pltpu.make_async_copy(src, dst, xs_recv.at[x])
            pl.when(own)(near.start)
            pl.when(jnp.logical_not(own))(far.start)
            shuffles.append((own, far))

    second_1 = pass_on(1)

    def arrived(copies):
        local, far = copies
        for copy in local:
            copy.wait()
        for copy in far:
            copy.wait_recv()

    def hidden(q):
        @pl.loop(0, 4)
        def _(n):
            rows = pl.ds(n * 256, 256)
            gate = up = None
            for s in range(RING):
                picked = tok[s, rows, :]
                w_gate = inbox[q * 8 + s].reshape(WIDE, COLS)
                w_up = inbox[q * 8 + 4 + s].reshape(WIDE, COLS)
                g = jnp.dot(picked, w_gate, preferred_element_type=F32)
                u = jnp.dot(picked, w_up, preferred_element_type=F32)
                gate, up = (g, u) if gate is None else (gate + g, up + u)
            hid2[q, rows, :] = ((up + 1.0) * gate * jax.nn.sigmoid(1.702 * gate)).astype(BF16)

    arrived(second_0)
    for copy in tok_far:
        copy.wait_recv()
    hidden(0)

    for n in range(RING):
        landed(xs.at[n], xs_recv.at[n])

    def down_first(r):
        local, far = [], []
        for step in (2, 1, 3, 0):
            yy, zz = ring(y, step), ring(z, step)
            rows = pl.ds(r * TILE, TILE)
            a = (xs.at[:, pl.ds(yy * 4, 4), rows], midd.at[0, r, :, y])
            b = (xs.at[:, pl.ds(16 + zz * 4, 4), rows], midd.at[1, r, :, z])
            if step == 0:
                local += [pltpu.make_async_copy(*pair, d1_recv.at[ab, r, 0]) for ab, pair in enumerate((a, b))]
                continue
            for ab, pair, target in ((0, a, device(yy, z, c, x)), (1, b, device(y, zz, c, x))):
                far.append(remote(*pair, d1_send.at[ab, r, step], d1_recv.at[ab, r, step], target))
        return local, far

    def down_second(r):
        local, far = [], []
        for step in (2, 1, 3, 0):
            yy, zz = ring(y, step), ring(z, step)
            a = (midd.at[0, r, :, :, zz], in_d[r].at[0, :, :, z])
            b = (midd.at[1, r, :, :, yy], in_d[r].at[1, :, y])
            if step == 0:
                local += [pltpu.make_async_copy(*pair, d2_recv.at[ab, r, 0]) for ab, pair in enumerate((a, b))]
                continue
            for ab, pair, target in ((0, a, device(y, zz, c, x)), (1, b, device(yy, z, c, x))):
                far.append(remote(*pair, d2_send.at[ab, r, step], d2_recv.at[ab, r, step], target))
        return local, far

    def start(copies):
        for copy in copies[1] + copies[0]:
            copy.start()

    down_1 = [down_first(r) for r in range(CHUNKS)]
    down_2 = [down_second(r) for r in range(CHUNKS)]
    for copies in down_1:
        start(copies)

    arrived(second_1)
    hidden(1)

    load_order = pltpu.make_async_copy(order, inbox, order_sem)
    load_order.start()

    lanes = lax.broadcasted_iota(jnp.int32, (BLOCK, TOK), 1)
    hid_near, hid_far = [], []
    for h in (0, 1):
        @pl.loop(0, 4)
        def _(n):
            slot = 2 * n + h
            pick = (sel[slot] == lanes).astype(F32).astype(BF16)
            hid[x, h, n] = jnp.dot(pick, hid2[expert[slot]], preferred_element_type=F32).astype(BF16)

        own, below, above = hid.at[x, h], hid.at[ring(x, 3), h, pl.ds(0, 2)], hid.at[ring(x, 1), h, pl.ds(2, 2)]
        hid_near.append([
            remote(own, own, hid_send.at[h, 0], hid_recv.at[h, 0], right),
            remote(own, own, hid_send.at[h, 1], hid_recv.at[h, 1], left),
        ])
        hid_far.append([
            remote(below, below, hid_send.at[h, 2], hid_recv.at[h, 2], right),
            remote(above, above, hid_send.at[h, 3], hid_recv.at[h, 3], left),
        ])
        for copy in hid_near[h]:
            copy.start()

    def hid_forward(h):
        for near, far in zip(hid_near[h], hid_far[h]):
            near.wait_recv()
            far.start()

    arrived(down_1[0])
    start(down_2[0])
    hid_forward(0)
    arrived(down_1[1])
    start(down_2[1])
    hid_forward(1)
    arrived(down_1[2])
    start(down_2[2])

    results = []

    def project(h, r):
        for step in (2, 1, 3, 0):
            to = ring(x, step)
            which = expert[2 * to + h]
            total = None
            for s in range(RING):
                part = lax.dot_general(
                    hid[s, h, to],
                    in_d[r][which, s].reshape(BLOCK, COLS),
                    (((1,), (1,)), ((), ())),
                    preferred_element_type=F32,
                )
                total = part if total is None else total + part
            if step == 0:
                fin[x, h, r] = total.astype(BF16)
                continue
            ob_out[step - 1, h, r] = total.astype(BF16)
            copy = remote(
                ob_out.at[step - 1, h, r], fin.at[x, h, r], out_send.at[h, r, step - 1], out_recv.at[h, r, step - 1],
                device(y, z, c, to),
            )
            copy.start()
            results.append((h, r, copy))

    for copy in hid_far[0]:
        copy.wait_recv()
    arrived(down_2[0])
    project(0, 0)
    arrived(down_2[1])
    project(0, 1)
    for copy in hid_far[1]:
        copy.wait_recv()
    project(1, 0)
    project(1, 1)
    arrived(down_2[2])
    project(0, 2)
    project(1, 2)

    load_order.wait()

    def ordered(h, half, matrix):
        lhs = jnp.concatenate(
            [fin[s, h, r, :, half * LANES : (half + 1) * LANES] for s in range(RING) for r in range(CHUNKS)], axis=1
        )
        return jnp.dot(lhs, inbox[pl.ds(2 * matrix, 2)].reshape(12 * LANES, OUTB), preferred_element_type=F32)

    for h in (0, 1):
        for hh, _, copy in results:
            if hh == h:
                copy.wait_recv()
        rows = slice(h * BLOCK, (h + 1) * BLOCK)

        @pl.loop(0, 3)
        def _(b):
            out[rows, pl.ds(pl.multiple_of(b * OUTB, OUTB), OUTB)] = ordered(h, 0, b).astype(BF16)

        out[rows, 3 * OUTB : 4 * OUTB] = (ordered(h, 0, 3) + ordered(h, 1, 8)).astype(BF16)

        @pl.loop(4, 7)
        def _(b):
            out[rows, pl.ds(pl.multiple_of(b * OUTB, OUTB), OUTB)] = ordered(h, 1, b).astype(BF16)

        out[rows, 7 * OUTB : D] = ordered(h, 1, 7)[:, : D - 7 * OUTB].astype(BF16)

    sent(1)
    for own, far in shuffles:
        pl.when(jnp.logical_not(own))(far.wait_send)
    for copies in (second_0, second_1, *down_1, *down_2):
        for copy in copies[1]:
            copy.wait_send()
    for copy in tok_near + tok_far + sum(hid_near + hid_far, []) + [copy for _, _, copy in results]:
        copy.wait_send()


def body(tokens, gate_weight, up_weight, down_weight, block_counts, block_tokens):
    total = jnp.sum(block_counts)
    slot = jnp.arange(SLOTS, dtype=jnp.int32)
    expert = (slot >= block_counts[0]).astype(jnp.int32)
    sel = jnp.where((slot < total)[:, None], block_tokens, -1)[:, :, None]
    split = (RING, RING, 2, 2, ROWS, COLS)
    vmem, hbm = pl.BlockSpec(memory_space=pltpu.VMEM), pl.BlockSpec(memory_space=pltpu.HBM)
    dma = pltpu.SemaphoreType.DMA
    made = pl.pallas_call(
        kernel,
        out_shape=(
            jax.ShapeDtypeStruct((2 * BLOCK, D), BF16),
            jax.ShapeDtypeStruct((2, 2, RING, 8, PAD, COLS), BF16),
            jax.ShapeDtypeStruct((RING, 32, 48, COLS), BF16),
            jax.ShapeDtypeStruct((2, CHUNKS, RING, RING, RING, TILE, COLS), BF16),
        ),
        in_specs=[vmem, hbm, hbm, hbm, vmem, pl.BlockSpec(memory_space=pltpu.SMEM), vmem, vmem, hbm],
        out_specs=(vmem, hbm, hbm, hbm),
        scratch_shapes=[
            pltpu.VMEM((2, 64, PAD, COLS), BF16),
            pltpu.VMEM((18, RING, 2, PAD, COLS), BF16),
            pltpu.VMEM((RING, TOK, WIDE), BF16),
            pltpu.VMEM((2, 2, RING, 2, ROWS, COLS), BF16),
            *[pltpu.VMEM((2, RING, RING, RING, TILE, COLS), BF16) for _ in range(CHUNKS)],
            pltpu.VMEM((2, TOK, COLS), BF16),
            pltpu.VMEM((RING, 2, RING, BLOCK, COLS), BF16),
            pltpu.VMEM((3, 2, CHUNKS, BLOCK, BLOCK), BF16),
            pltpu.VMEM((RING, 2, CHUNKS, BLOCK, BLOCK), BF16),
            dma((2, 2)),
            dma,
            dma((2, 2, RING)), dma((2, 2, RING)),
            dma((2, 2, RING, 2)), dma((2, 2, RING, 2)),
            dma((2, 2)), dma((RING,)),
            dma((2, CHUNKS, RING)), dma((2, CHUNKS, RING)),
            dma((2, CHUNKS, RING)), dma((2, CHUNKS, RING)),
            dma((RING,)), dma((RING,)),
            dma((2, RING)), dma((2, RING)),
            dma((2, CHUNKS, 3)), dma((2, CHUNKS, 3)),
        ],
        compiler_params=pltpu.CompilerParams(
            collective_id=0, has_side_effects=True, vmem_limit_bytes=60 * 2**20
        ),
    )(
        tokens,
        gate_weight.reshape(split),
        up_weight.reshape(split),
        down_weight.reshape(split),
        sel,
        expert,
        jnp.asarray(place_matrix(), BF16),
        jnp.asarray(group_matrix(), BF16),
        jnp.asarray(order_matrix(), BF16).reshape(18, RING, 2, PAD, COLS),
    )
    return made[0]


def solution(mesh):
    in_specs = (
        P("expert", "shard"),
        P(None, "expert", "shard"),
        P(None, "expert", "shard"),
        P(None, "expert", "shard"),
        P("expert"),
        P("expert", None),
    )
    out_specs = P(("expert", "shard"), None)
    return jax.shard_map(body, mesh=mesh, in_specs=in_specs, out_specs=out_specs, check_vma=False)
```

time: 836 us -> 252 us (0.30); the launches traced: 826 us -> 252 us
  waiting for transfers between devices: 238 us -> 0 us
  local copies, waits for them, and re-layouts: 255 us -> 25.4 us
  Pallas kernels: 0 us -> 222 us
  other arithmetic: 125 us -> 3.88 us
  loops' own time: 71.4 us -> 0 us
  matrix products: 64.3 us -> 0 us
  starting transfers between devices: 58.5 us -> 0 us
  between operations: 13.8 us -> 0.03 us
    pallas_call x0 -> x1, Pallas kernels: none -> 222 us  [body(): pl.pallas_call(kernel, out_shape=(jax.ShapeDtypeStruct((2 * BLOCK, D), BF...]
    all_to_all x6 -> x0, waiting for transfers between devices: 130 us -> none  [the longest x1 61.8 us: body(): lax.all_to_all(coded_up, 'expert', split_axis=0, concat_axis=1, tiled=True)]
    convert_element_type x13 -> x0, local copies, waits for them, and re-layouts: 113 us -> none  [the longest x6 102 us: decode(): coded.astype(jnp.float32) * scales.astype(jnp.float32)[..., None]]
    reduce_scatter x1 -> x0, waiting for transfers between devices: 108 us -> none  [body(): lax.psum_scatter(made.reshape(lax.axis_size('shard') * own_rows, width).a...]
    convert_element_type x12 -> x1, other arithmetic: 101 us -> 1.17 us  [body(): expert = (slot >= block_counts[0]).astype(jnp.int32)]
    another operation x18 -> x0, loops' own time: 71.4 us -> none  [the longest x1 20.3 us: body(): hidden = lax.map(slot, jnp.arange(slots, dtype=jnp.int32))]
    dot_general x24 -> x0, matrix products: 64.3 us -> none  [the longest x8 21.6 us: project_work(): lax.dot_general(rows_hidden, w_down[local], (((1,), (1,)), ((), ())), pre...]
    all_to_all x6 -> x0, starting transfers between devices: 58.2 us -> none  [the longest x1 14.6 us: body(): lax.all_to_all(coded_gate, 'expert', split_axis=0, concat_axis=1, tiled=T...]
  transfers between devices with their start and end apart: 8 -> 0, of which waited for: 4 -> 0; matrix products, arithmetic and copies ran while one was open for 30% -> 0% of each run, Pallas kernels for 0% -> 0%
where the time goes in v1:
time: 252 us
  Pallas kernels  222 us (88%)
  local copies, waits for them, and re-layouts  25.4 us (10%)
  other arithmetic  3.88 us (2%)
    pallas_call x1, Pallas kernels, body(): pl.pallas_call(kernel, out_shape=(jax.ShapeDtypeStruct((2 * BLOCK, D), BF...  222 us
    unnamed x12, local copies, waits for them, and re-layouts  19.5 us

profile of v1, /device:TPU:1, one launch (start us, length us, event | category | flops | bytes accessed | tf_op | source)
XLA Modules:
  0.0 251.7 jit_solution(12039592653718018708)
XLA Ops:
  0.0 1.3 reduce_sum.9
  1.3 0.6 iota_compare_fusion
  1.9 1.2 compare_convert_fusion.expert
  3.1 0.8 select_bitcast_fusion
  3.9 1.4 copy.19.sel
  5.2 0.0 slice-start
  5.3 2.6 %copy.18.tokens = bf16[1024,720]{1,0:T(8,128)(2,1)} copy(bf16[1024,720]{0,1:T(8,128)(2,1)} %param.9) | data formatting | bytes 2949120 | tf_op args[0]
  7.9 0.0 slice-start.1
  7.9 0.0 slice-start.2
  7.9 7.3 %copy.15 = bf16[64,90,384]{2,1,0:T(8,128)(2,1)} copy(bf16[64,90,384]{2,0,1:T(8,128)(2,1)} %param.10) | data formatting | bytes 8847360 | tf_op args[1]
  15.1 0.0 slice-start.3
  15.1 0.0 slice-done
  15.1 0.0 slice-done.1
  15.1 4.8 %copy.16 = bf16[64,90,384]{2,1,0:T(8,128)(2,1)} copy(bf16[64,90,384]{2,0,1:T(8,128)(2,1)S(1)} %bitcast.11) | data formatting | bytes 8847360 | tf_op args[2]
  19.9 0.0 slice-done.2
  19.9 0.0 slice-done.3
  19.9 4.8 %copy.17 = bf16[64,90,384]{2,1,0:T(8,128)(2,1)} copy(bf16[64,90,384]{2,0,1:T(8,128)(2,1)S(1)} %bitcast.13) | data formatting | bytes 8847360 | tf_op args[3]
  24.7 222.4 %shard_map.91 = (bf16[512,2880]{1,0:T(8,128)(2,1)}, bf16[2,2,4,8,96,384]{5,4,3,2,1,0:T(8,128)(2,1)}, bf16[4,32,48,384]{3,2,1,0:T(8,128)(2,1)}, bf16[2,3,4,4,4,16,384]{6,5,4,3,2,1,0:T(8,128)(2,1)}) custom-call(bf16[1024,720]{1,0:T(8,128)(2,1)} %copy.18.tokens, bf16[4,4,2,2,90,384]{5,4,3,2,1,0:T(8,128)(2,1)} %bitcast.7, ...), custom_call_target="tpu_custom_call" | custom-call | tf_op jit(solution)/shard_map/pallas_call | solution.py:451
  247.1 4.6 %copy.20 = bf16[512,2880]{0,1:T(8,128)(2,1)} copy(bf16[512,2880]{1,0:T(8,128)(2,1)} %get-tuple-element.6) | data formatting | bytes 5898240 | tf_op jit(solution)/shard_map/pallas_call | solution.py:451
  (2 shorter events, 0.0 us)
Async XLA Ops:
  5.2 9.9 %slice-start = ((s8[4423680]{0:T(1024)(128)(4,1)}), s8[229376]{0:T(1024)(128)(4,1)S(1)}, s32[]{:S(2)}) async-start(s8[4423680]{0:T(1024)(128)(4,1)} %bitcast.10), calls=%async_computation | async-start | bytes 458752
  7.9 7.3 %slice-start.1 = ((s8[4423680]{0:T(1024)(128)(4,1)}), s8[4194304]{0:T(1024)(128)(4,1)S(1)}, s32[]{:S(2)}) async-start(s8[4423680]{0:T(1024)(128)(4,1)} %bitcast.10), calls=%async_computation.1 | async-start | bytes 8388608
  7.9 12.0 %slice-start.2 = ((s8[4423680]{0:T(1024)(128)(4,1)}), s8[4194304]{0:T(1024)(128)(4,1)S(1)}, s32[]{:S(2)}) async-start(s8[4423680]{0:T(1024)(128)(4,1)} %bitcast.12), calls=%async_computation.2 | async-start | bytes 8388608
  15.1 4.8 %slice-start.3 = ((s8[4423680]{0:T(1024)(128)(4,1)}), s8[229376]{0:T(1024)(128)(4,1)S(1)}, s32[]{:S(2)}) async-start(s8[4423680]{0:T(1024)(128)(4,1)} %bitcast.12), calls=%async_computation.3 | async-start | bytes 458752

commit v2 on v1

v2 whole, which is shorter than its diff:
```python
import functools

import jax
import jax.numpy as jnp
import numpy as np
from jax import lax
from jax.experimental import pallas as pl
from jax.experimental.pallas import tpu as pltpu
from jax.sharding import PartitionSpec as P

GROUP = 32
LANES = 128
BF16 = jnp.bfloat16
F32 = jnp.float32
MESH = pl.DeviceIdType.MESH

RING = 4
D = 2880
ROWS = 90
PAD = 96
FEAT = 720
WIDE = 8 * PAD
COLS = 384
TOK = 1024
BLOCK = 256
SLOTS = 8
TILE = 16
CHUNKS = 3
OUTB = 384


def place_matrix():
    m = np.zeros((FEAT, WIDE), np.float32)
    for k in range(FEAT):
        j, row = divmod(k, ROWS)
        m[k, row // 48 * (WIDE // 2) + j * 48 + row % 48] = 1
    return m


def group_matrix():
    lane = np.arange(LANES) // GROUP
    return (lane[:, None] == lane[None, :]).astype(np.float32)


def swap_matrix():
    m = np.zeros((BLOCK, BLOCK), np.float32)
    for k in range(BLOCK):
        m[k, k % 16 * 16 + k // 16] = 1
    return m


def order_matrix():
    m = np.zeros((9, RING, OUTB, OUTB), np.float32)
    for d in range(D):
        pair, rest = divmod(d, 2 * ROWS)
        core, row = divmod(rest, ROWS)
        part, row = divmod(row, 48)
        chunk, row = divmod(row, TILE)
        half, pair = divmod(pair, 8)
        block, col = divmod(d, OUTB)
        if block == 3 and half == 1:
            block = 8
        m[block, 2 * core + part, col, chunk * LANES + pair * TILE + row] = 1
    return m


def power_floor(value):
    far = value * 8388609.0
    return far - (far - value)


def restore(weight, groups):
    power = power_floor(jnp.abs(weight) * 0.751953125)
    square = power * power
    sixth = (square * square) * (square * 2.0**60)
    total = jnp.dot(sixth.astype(BF16), groups, preferred_element_type=F32)
    top = power_floor(jnp.exp2((jnp.log2(total) - 60.0) * (1.0 / 6.0)) * 0.8)
    top = jnp.minimum(jnp.maximum(top, 2.0**-30), 2.0**8)
    magic = jnp.maximum(power, top * 0.25) * (1.5 * 2.0**22)
    rounded = (weight + magic) - magic
    limit = top * 1.5
    return jnp.minimum(jnp.maximum(rounded, -limit), limit).astype(BF16)


def kernel(
    tokens, gate_w, up_w, down_w, block_tokens, counts, place, groups, swap, order,
    out, mid, xs, midd,
    ob, inbox, tok, stage, in_0, in_1, in_2, hid2, hid, ob_out, fin, picks, sums,
    stage_sem, order_sem, s1_send, s1_recv, s2_send, s2_recv, xs_send, xs_recv,
    d1_send, d1_recv, d2_send, d2_recv, tok_send, tok_recv, hid_send, hid_recv, out_send, out_recv,
):
    in_d = (in_0, in_1, in_2)
    me, x = lax.axis_index("expert"), lax.axis_index("shard")
    y, z, c = me // 8, (me // 2) % 4, me % 2

    def device(yy, zz, cc, xx):
        return ((yy * 4 + zz) * 2 + cc, xx)

    def ring(at, step):
        return (at + step) % RING

    def remote(src, dst, send, recv, target):
        return pltpu.make_async_remote_copy(
            src_ref=src, dst_ref=dst, send_sem=send, recv_sem=recv, device_id=target, device_id_type=MESH
        )

    def landed(ref, sem):
        pltpu.make_async_copy(ref, ref, sem).wait()

    barrier = pltpu.get_barrier_semaphore()
    peers = [device(y, z, 1 - c, x)]
    for step in (1, 2, 3):
        for cc in (c, 1 - c):
            peers += [device(ring(y, step), z, cc, x), device(y, ring(z, step), cc, x), device(y, z, cc, ring(x, step))]
    for peer in peers:
        pl.semaphore_signal(barrier, inc=1, device_id=peer, device_id_type=MESH)

    def load(weight, q, yy, slot, ab):
        experts = pl.ds(yy * 16, 16)
        main = pltpu.make_async_copy(
            weight.at[pl.ds(q * 48, 42), experts], stage.at[slot, ab, 0:42], stage_sem.at[slot, ab, 0]
        )
        rest = pltpu.make_async_copy(weight.at[42:48, experts], stage.at[slot, ab, 42:48], stage_sem.at[slot, ab, 1])
        return main, rest

    def load_start(weight, q, yy, slot, ab):
        main, rest = load(weight, q, yy, slot, ab)
        main.start()
        pl.when(q == 0)(rest.start)

    def load_wait(weight, q, yy, slot, ab):
        main, rest = load(weight, q, yy, slot, ab)
        main.wait()
        pl.when(q == 0)(rest.wait)

        @pl.when(q == 1)
        def _():
            stage[slot, ab, 42:48] = jnp.zeros((6, 16, COLS), BF16)

    load_start(gate_w, 0, ring(y, 1), 0, 0)
    load_start(up_w, 0, 0, 0, 1)
    picks[...] = jnp.transpose(block_tokens[...])

    @pl.loop(0, 4)
    def _(n):
        rows = pl.ds(pl.multiple_of(n * 256, 256), 256)
        tok[x, rows, :] = lax.dot_general(
            tokens[:, rows], place[...], (((0,), (0,)), ((), ())), preferred_element_type=F32
        ).astype(BF16)

    pl.semaphore_wait(barrier, len(peers))

    right, left = device(y, z, c, ring(x, 1)), device(y, z, c, ring(x, 3))
    tok_near = [
        remote(tok.at[x], tok.at[x], tok_send.at[0], tok_recv.at[0], right),
        remote(tok.at[x], tok.at[x], tok_send.at[1], tok_recv.at[1], left),
    ]
    for copy in tok_near:
        copy.start()
    lower, upper = pl.ds(0, 512), pl.ds(512, 512)
    tok_far = [
        remote(tok.at[ring(x, 3), lower], tok.at[ring(x, 3), lower], tok_send.at[2], tok_recv.at[2], right),
        remote(tok.at[ring(x, 1), upper], tok.at[ring(x, 1), upper], tok_send.at[3], tok_recv.at[3], left),
    ]

    def encode(slot, ab, to):
        @pl.loop(0, 3, unroll=3)
        def _(j):
            rows = pl.ds(pl.multiple_of(j * TILE, TILE), TILE)
            for lane in range(COLS // LANES):
                cols = slice(lane * LANES, (lane + 1) * LANES)
                block = stage[slot, ab, rows, :, cols].reshape(BLOCK, LANES)
                for zz in range(RING):
                    weight = jnp.dot(swap[zz * 64 : zz * 64 + 64, :], block, preferred_element_type=F32)
                    ob[*to, zz, :, :, rows, cols] = restore(weight, groups[...]).reshape(2, 2, TILE, LANES)

    def first_y(q, step):
        to = ring(y, step)
        return ob.at[0, q, to], mid.at[0, q, y], s1_send.at[0, q, step], s1_recv.at[0, q, step], device(to, z, c, x)

    def first_z(q, step, yy):
        to = ring(z, step)
        send, recv = s1_send.at[1, q, step], s1_recv.at[1, q, step]
        return ob.at[1, q, yy, to], mid.at[1, q, z, yy], send, recv, device(y, to, c, x)

    @pl.loop(0, 8)
    def _(n):
        slot, q, i = n % 2, n // 4, n % 4
        load_wait(gate_w, q, ring(y, i + 1), slot, 0)
        load_wait(up_w, q, i, slot, 1)

        @pl.when(n < 7)
        def _():
            load_start(gate_w, (n + 1) // 4, ring(y, n + 2), 1 - slot, 0)
            load_start(up_w, (n + 1) // 4, (n + 1) % 4, 1 - slot, 1)

        encode(slot, 0, (0, q, ring(y, i + 1)))

        @pl.when(i == 3)
        def _():
            src, dst, _, recv, _ = first_y(q, 0)
            pltpu.make_async_copy(src, dst, recv).start()

        @pl.when(i != 3)
        def _():
            remote(*first_y(q, i + 1)).start()

        encode(slot, 1, (1, q, i))
        for step in (2, 1, 3):
            remote(*first_z(q, step, i)).start()
        src, dst, _, recv, _ = first_z(q, 0, i)
        pltpu.make_async_copy(src, dst, recv).start()

    load_start(down_w, 0, 0, 0, 0)
    everything = slice(None)

    def second(q):
        local, far = [], []
        rows = pl.ds(q * 48, 48)
        for step in (2, 1, 3, 0):
            for dc in (0, 1):
                cc = (c + dc) % 2
                zz, yy = ring(z, step), ring(y, step)
                a = (mid.at[0, q, :, zz, cc], inbox.at[0:4, z, c, :, rows])
                b = (mid.at[1, q, :, yy, cc], inbox.at[4 + y, :, c, :, rows])
                if step == 0 and dc == 0:
                    local += [pltpu.make_async_copy(*pair, s2_recv.at[ab, q, 0, 0]) for ab, pair in enumerate((a, b))]
                    continue
                for ab, pair, target in ((0, a, device(y, zz, cc, x)), (1, b, device(yy, z, cc, x))):
                    far.append(remote(*pair, s2_send.at[ab, q, step, dc], s2_recv.at[ab, q, step, dc], target))
        return local, far

    def pass_on(q):
        for step in range(RING):
            landed(mid.at[0, q, y], s1_recv.at[0, q, step])
            landed(mid.at[1, q, z], s1_recv.at[1, q, step])
        local, far = second(q)
        for copy in far + local:
            copy.start()
        return local, far

    def sent(q):
        for step in (1, 2, 3):
            remote(*first_y(q, step)).wait_send()
            remote(*first_z(q, step, everything)).wait_send()

    second_0 = pass_on(0)
    for near, far in zip(tok_near, tok_far):
        near.wait_recv()
        far.start()

    sent(0)

    @pl.loop(0, 8)
    def _(n):
        slot, h, yy = n % 2, n // 4, n % 4
        load_wait(down_w, h, yy, slot, 0)

        @pl.when(n < 7)
        def _():
            load_start(down_w, (n + 1) // 4, (n + 1) % 4, 1 - slot, 0)

        encode(slot, 0, (h, 0, yy))

    shuffles = []
    for cc in (0, 1):
        for h in (0, 1):
            to = 2 * c + h
            src, dst = ob.at[h, 0, :, :, cc], xs.at[x]
            own = jnp.logical_and(cc == c, to == x)
            far = remote(src, dst, xs_send.at[cc, h], xs_recv.at[x], device(y, z, cc, to))
            near = pltpu.make_async_copy(src, dst, xs_recv.at[x])
            pl.when(own)(near.start)
            pl.when(jnp.logical_not(own))(far.start)
            shuffles.append((own, far))

    second_1 = pass_on(1)

    def arrived(copies):
        local, far = copies
        for copy in local:
            copy.wait()
        for copy in far:
            copy.wait_recv()

    def products(q):
        @pl.loop(0, 8)
        def _(n):
            e, rows = n // 4, pl.ds(pl.multiple_of(n % 4 * 256, 256), 256)
            made = []
            for ab in (0, 1):
                total = None if q == 0 else sums[e, ab, rows, :]
                for s in range(RING):
                    weight = inbox[4 * ab + s, :, :, e, q * 48 : q * 48 + 48].reshape(WIDE // 2, COLS)
                    picked = tok[s, rows, q * (WIDE // 2) : (q + 1) * (WIDE // 2)]
                    part = jnp.dot(picked, weight, preferred_element_type=F32)
                    total = part if total is None else total + part
                made.append(total)
            if q == 0:
                sums[e, 0, rows, :], sums[e, 1, rows, :] = made
            else:
                gate, up = made
                hid2[e, rows, :] = ((up + 1.0) * gate * jax.nn.sigmoid(1.702 * gate)).astype(BF16)

    arrived(second_0)
    for copy in tok_far:
        copy.wait_recv()
    products(0)

    for n in range(RING):
        landed(xs.at[n], xs_recv.at[n])

    def down_first(r):
        local, far = [], []
        for step in (2, 1, 3, 0):
            yy, zz = ring(y, step), ring(z, step)
            rows = pl.ds(r * TILE, TILE)
            a = (xs.at[:, yy, :, 0, rows], midd.at[0, r, :, y])
            b = (xs.at[:, :, zz, 1, rows], midd.at[1, r, :, z])
            if step == 0:
                local += [pltpu.make_async_copy(*pair, d1_recv.at[ab, r, 0]) for ab, pair in enumerate((a, b))]
                continue
            for ab, pair, target in ((0, a, device(yy, z, c, x)), (1, b, device(y, zz, c, x))):
                far.append(remote(*pair, d1_send.at[ab, r, step], d1_recv.at[ab, r, step], target))
        return local, far

    def down_second(r):
        local, far = [], []
        for step in (2, 1, 3, 0):
            yy, zz = ring(y, step), ring(z, step)
            a = (midd.at[0, r, :, :, zz], in_d[r].at[0, :, :, z])
            b = (midd.at[1, r, :, :, yy], in_d[r].at[1, :, y])
            if step == 0:
                local += [pltpu.make_async_copy(*pair, d2_recv.at[ab, r, 0]) for ab, pair in enumerate((a, b))]
                continue
            for ab, pair, target in ((0, a, device(y, zz, c, x)), (1, b, device(yy, z, c, x))):
                far.append(remote(*pair, d2_send.at[ab, r, step], d2_recv.at[ab, r, step], target))
        return local, far

    def start(copies):
        for copy in copies[1] + copies[0]:
            copy.start()

    down_1 = [down_first(r) for r in range(CHUNKS)]
    down_2 = [down_second(r) for r in range(CHUNKS)]
    for copies in down_1:
        start(copies)

    arrived(second_1)
    products(1)

    load_order = pltpu.make_async_copy(order, inbox, order_sem)
    load_order.start()

    first, total = counts[0], counts[0] + counts[1]
    lanes = lax.broadcasted_iota(jnp.int32, (BLOCK, TOK), 1)
    hid_near, hid_far = [], []
    for h in (0, 1):
        for n in range(RING):
            slot = 2 * n + h
            row = jnp.where(slot < total, picks[:, slot : slot + 1], -1)
            pick = (row == lanes).astype(F32).astype(BF16)
            which = (slot >= first).astype(jnp.int32)
            hid[x, h, n] = jnp.dot(pick, hid2[which], preferred_element_type=F32).astype(BF16)

        own, below, above = hid.at[x, h], hid.at[ring(x, 3), h, pl.ds(0, 2)], hid.at[ring(x, 1), h, pl.ds(2, 2)]
        hid_near.append([
            remote(own, own, hid_send.at[h, 0], hid_recv.at[h, 0], right),
            remote(own, own, hid_send.at[h, 1], hid_recv.at[h, 1], left),
        ])
        hid_far.append([
            remote(below, below, hid_send.at[h, 2], hid_recv.at[h, 2], right),
            remote(above, above, hid_send.at[h, 3], hid_recv.at[h, 3], left),
        ])
        for copy in hid_near[h]:
            copy.start()

    def hid_forward(h):
        for near, far in zip(hid_near[h], hid_far[h]):
            near.wait_recv()
            far.start()

    arrived(down_1[0])
    start(down_2[0])
    hid_forward(0)
    arrived(down_1[1])
    start(down_2[1])
    hid_forward(1)
    arrived(down_1[2])
    start(down_2[2])

    results = []

    def project(h, r):
        for step in (2, 1, 3, 0):
            to = ring(x, step)
            which = (2 * to + h >= first).astype(jnp.int32)
            made = None
            for s in range(RING):
                part = lax.dot_general(
                    hid[s, h, to],
                    in_d[r][which, s].reshape(BLOCK, COLS),
                    (((1,), (1,)), ((), ())),
                    preferred_element_type=F32,
                )
                made = part if made is None else made + part
            if step == 0:
                fin[x, h, r] = made.astype(BF16)
                continue
            ob_out[step - 1, h, r] = made.astype(BF16)
            copy = remote(
                ob_out.at[step - 1, h, r], fin.at[x, h, r], out_send.at[h, r, step - 1], out_recv.at[h, r, step - 1],
                device(y, z, c, to),
            )
            copy.start()
            results.append((h, r, copy))

    for copy in hid_far[0]:
        copy.wait_recv()
    arrived(down_2[0])
    project(0, 0)
    arrived(down_2[1])
    project(0, 1)
    for copy in hid_far[1]:
        copy.wait_recv()
    project(1, 0)
    project(1, 1)
    arrived(down_2[2])
    project(0, 2)
    project(1, 2)

    load_order.wait()

    def ordered(h, half, matrix):
        result = None
        table = inbox[matrix].reshape(RING * OUTB, OUTB)
        for n in range(RING):
            got = [fin[n, h, r, :, half * LANES : (half + 1) * LANES] for r in range(CHUNKS)]
            part = lax.dot_general(
                table[n * OUTB : (n + 1) * OUTB],
                jnp.concatenate(got, axis=1),
                (((1,), (1,)), ((), ())),
                preferred_element_type=F32,
            )
            result = part if result is None else result + part
        return result

    for h in (0, 1):
        for hh, _, copy in results:
            if hh == h:
                copy.wait_recv()
        rows = slice(h * BLOCK, (h + 1) * BLOCK)

        @pl.loop(0, 3)
        def _(b):
            out[pl.ds(pl.multiple_of(b * OUTB, OUTB), OUTB), rows] = ordered(h, 0, b).astype(BF16)

        out[3 * OUTB : 4 * OUTB, rows] = (ordered(h, 0, 3) + ordered(h, 1, 8)).astype(BF16)

        @pl.loop(4, 7)
        def _(b):
            out[pl.ds(pl.multiple_of(b * OUTB, OUTB), OUTB), rows] = ordered(h, 1, b).astype(BF16)

        out[7 * OUTB : D, rows] = ordered(h, 1, 7)[: D - 7 * OUTB].astype(BF16)

    sent(1)
    for own, far in shuffles:
        pl.when(jnp.logical_not(own))(far.wait_send)
    for copies in (second_0, second_1, *down_1, *down_2):
        for copy in copies[1]:
            copy.wait_send()
    for copy in tok_near + tok_far + sum(hid_near + hid_far, []) + [copy for _, _, copy in results]:
        copy.wait_send()


def body(tokens, gate_weight, up_weight, down_weight, block_counts, block_tokens):
    vmem, hbm = pl.BlockSpec(memory_space=pltpu.VMEM), pl.BlockSpec(memory_space=pltpu.HBM)
    dma = pltpu.SemaphoreType.DMA
    made = pl.pallas_call(
        kernel,
        out_shape=(
            jax.ShapeDtypeStruct((D, 2 * BLOCK), BF16),
            jax.ShapeDtypeStruct((2, 2, RING, RING, 2, 2, 48, COLS), BF16),
            jax.ShapeDtypeStruct((RING, RING, RING, 2, 48, COLS), BF16),
            jax.ShapeDtypeStruct((2, CHUNKS, RING, RING, RING, TILE, COLS), BF16),
        ),
        in_specs=[vmem, hbm, hbm, hbm, vmem, pl.BlockSpec(memory_space=pltpu.SMEM), vmem, vmem, vmem, hbm],
        out_specs=(vmem, hbm, hbm, hbm),
        scratch_shapes=[
            pltpu.VMEM((2, 2, RING, RING, 2, 2, 48, COLS), BF16),
            pltpu.VMEM((9, RING, 2, 2, PAD, COLS), BF16),
            pltpu.VMEM((RING, TOK, WIDE), BF16),
            pltpu.VMEM((2, 2, 48, 16, COLS), BF16),
            *[pltpu.VMEM((2, RING, RING, RING, TILE, COLS), BF16) for _ in range(CHUNKS)],
            pltpu.VMEM((2, TOK, COLS), BF16),
            pltpu.VMEM((RING, 2, RING, BLOCK, COLS), BF16),
            pltpu.VMEM((3, 2, CHUNKS, BLOCK, BLOCK), BF16),
            pltpu.VMEM((RING, 2, CHUNKS, BLOCK, BLOCK), BF16),
            pltpu.VMEM((BLOCK, SLOTS), jnp.int32),
            pltpu.VMEM((2, 2, TOK, COLS), F32),
            dma((2, 2, 2)),
            dma,
            dma((2, 2, RING)), dma((2, 2, RING)),
            dma((2, 2, RING, 2)), dma((2, 2, RING, 2)),
            dma((2, 2)), dma((RING,)),
            dma((2, CHUNKS, RING)), dma((2, CHUNKS, RING)),
            dma((2, CHUNKS, RING)), dma((2, CHUNKS, RING)),
            dma((RING,)), dma((RING,)),
            dma((2, RING)), dma((2, RING)),
            dma((2, CHUNKS, 3)), dma((2, CHUNKS, 3)),
        ],
        compiler_params=pltpu.CompilerParams(
            collective_id=0, has_side_effects=True, vmem_limit_bytes=60 * 2**20
        ),
    )(
        tokens.T,
        *[jnp.swapaxes(weight, 0, 1) for weight in (gate_weight, up_weight, down_weight)],
        block_tokens,
        block_counts,
        jnp.asarray(place_matrix(), BF16),
        jnp.asarray(group_matrix(), BF16),
        jnp.asarray(swap_matrix(), BF16),
        jnp.asarray(order_matrix(), BF16).reshape(9, RING, 2, 2, PAD, COLS),
    )
    return made[0].T


def solution(mesh):
    in_specs = (
        P("expert", "shard"),
        P(None, "expert", "shard"),
        P(None, "expert", "shard"),
        P(None, "expert", "shard"),
        P("expert"),
        P("expert", None),
    )
    out_specs = P(("expert", "shard"), None)
    return jax.shard_map(body, mesh=mesh, in_specs=in_specs, out_specs=out_specs, check_vma=False)
```

time: 252 us -> 226 us (0.90)
  local copies, waits for them, and re-layouts: 25.4 us -> 3.62 us
  other arithmetic: 3.88 us -> 0 us
    unnamed x12 -> x1, local copies, waits for them, and re-layouts: 19.5 us -> 3.62 us
    pallas_call x1 -> x0, local copies, waits for them, and re-layouts: 4.57 us -> none  [body(): pl.pallas_call(kernel, out_shape=(jax.ShapeDtypeStruct((2 * BLOCK, D), BF...]
where the time goes in v2:
time: 226 us
  Pallas kernels  223 us (99%)
  local copies, waits for them, and re-layouts  3.62 us (2%)
    pallas_call x1, Pallas kernels, body(): pl.pallas_call(kernel, out_shape=(jax.ShapeDtypeStruct((D, 2 * BLOCK), BF...  223 us

profile of v2, /device:TPU:1, one launch (start us, length us, event | category | flops | bytes accessed | tf_op | source)
XLA Modules:
  0.0 226.2 jit_solution(8508858451087275876)
XLA Ops:
  0.0 222.6 %shard_map.100 = (bf16[2880,512]{1,0:T(8,128)(2,1)}, bf16[2,2,4,4,2,2,48,384]{7,6,5,4,3,2,1,0:T(8,128)(2,1)}, bf16[4,4,4,2,48,384]{5,4,3,2,1,0:T(8,128)(2,1)}, bf16[2,3,4,4,4,16,384]{6,5,4,3,2,1,0:T(8,128)(2,1)}) custom-call(bf16[720,1024]{1,0:T(8,128)(2,1)} %bitcast.9, bf16[90,64,384]{2,1,0:T(8,128)(2,1)} %bitcast.5, bf16[90,64,384]{2,1,0:T(8,128)(2,1)} %bitcast.6, ...), custom_call_target="tpu_custom_call" | custom-call | tf_op jit(solution)/shard_map/pallas_call | solution.py:479
  222.6 3.6 %copy.12 = bf16[512,2880]{0,1:T(8,128)(2,1)} copy(bf16[512,2880]{0,1:T(8,128)(2,1)} %bitcast.8) | data formatting | bytes 5898240

commit v3 on v2

--- a/solution.py
+++ b/solution.py
@@ -32,8 +32,7 @@
 def place_matrix():
     m = np.zeros((FEAT, WIDE), np.float32)
     for k in range(FEAT):
-        j, row = divmod(k, ROWS)
-        m[k, row // 48 * (WIDE // 2) + j * 48 + row % 48] = 1
+        m[k, k // ROWS * PAD + k % ROWS] = 1
     return m
 
 
@@ -43,9 +42,10 @@
 
 
 def swap_matrix():
-    m = np.zeros((BLOCK, BLOCK), np.float32)
-    for k in range(BLOCK):
-        m[k, k % 16 * 16 + k // 16] = 1
+    m = np.zeros((2, LANES, BLOCK), np.float32)
+    for e in range(2):
+        for k in range(LANES):
+            m[e, k, k % 16 * 16 + k // 16 * 2 + e] = 1
     return m
 
 
@@ -84,9 +84,9 @@
 
 def kernel(
     tokens, gate_w, up_w, down_w, block_tokens, counts, place, groups, swap, order,
-    out, mid, xs, midd,
-    ob, inbox, tok, stage, in_0, in_1, in_2, hid2, hid, ob_out, fin, picks, sums,
-    stage_sem, order_sem, s1_send, s1_recv, s2_send, s2_recv, xs_send, xs_recv,
+    out, mid, xs, midd, raw,
+    ob, inbox, tok, stage, in_0, in_1, in_2, hid, picked, ob_out, fin, picks, shown,
+    stage_sem, order_sem, shown_sem, s1_send, s1_recv, s2_send, s2_recv, xs_send, xs_recv,
     d1_send, d1_recv, d2_send, d2_recv, tok_send, tok_recv, hid_send, hid_recv, out_send, out_recv,
 ):
     in_d = (in_0, in_1, in_2)
@@ -115,64 +115,43 @@
     for peer in peers:
         pl.semaphore_signal(barrier, inc=1, device_id=peer, device_id_type=MESH)
 
-    def load(weight, q, yy, slot, ab):
-        experts = pl.ds(yy * 16, 16)
-        main = pltpu.make_async_copy(
-            weight.at[pl.ds(q * 48, 42), experts], stage.at[slot, ab, 0:42], stage_sem.at[slot, ab, 0]
+    def load(weight, yy, slot, ab):
+        return pltpu.make_async_copy(
+            weight.at[:, pl.ds(yy * 16, 16)], stage.at[slot, ab, 0:ROWS], stage_sem.at[slot, ab]
         )
-        rest = pltpu.make_async_copy(weight.at[42:48, experts], stage.at[slot, ab, 42:48], stage_sem.at[slot, ab, 1])
-        return main, rest
-
-    def load_start(weight, q, yy, slot, ab):
-        main, rest = load(weight, q, yy, slot, ab)
-        main.start()
-        pl.when(q == 0)(rest.start)
-
-    def load_wait(weight, q, yy, slot, ab):
-        main, rest = load(weight, q, yy, slot, ab)
-        main.wait()
-        pl.when(q == 0)(rest.wait)
-
-        @pl.when(q == 1)
-        def _():
-            stage[slot, ab, 42:48] = jnp.zeros((6, 16, COLS), BF16)
-
-    load_start(gate_w, 0, ring(y, 1), 0, 0)
-    load_start(up_w, 0, 0, 0, 1)
-    picks[...] = jnp.transpose(block_tokens[...])
-
-    @pl.loop(0, 4)
-    def _(n):
-        rows = pl.ds(pl.multiple_of(n * 256, 256), 256)
-        tok[x, rows, :] = lax.dot_general(
-            tokens[:, rows], place[...], (((0,), (0,)), ((), ())), preferred_element_type=F32
-        ).astype(BF16)
+
+    load(gate_w, ring(y, 1), 0, 0).start()
+    load(up_w, 0, 0, 1).start()
+    stage[:, :, ROWS:PAD] = jnp.zeros((2, 2, PAD - ROWS, 16, COLS), BF16)
+    turned = jnp.transpose(block_tokens[...])
+    for n in range(SLOTS):
+        picks[n] = jnp.broadcast_to(turned[:, n : n + 1], (BLOCK, LANES))
 
     pl.semaphore_wait(barrier, len(peers))
 
     right, left = device(y, z, c, ring(x, 1)), device(y, z, c, ring(x, 3))
     tok_near = [
-        remote(tok.at[x], tok.at[x], tok_send.at[0], tok_recv.at[0], right),
-        remote(tok.at[x], tok.at[x], tok_send.at[1], tok_recv.at[1], left),
+        remote(tokens, raw.at[x], tok_send.at[0], tok_recv.at[0], right),
+        remote(tokens, raw.at[x], tok_send.at[1], tok_recv.at[1], left),
     ]
     for copy in tok_near:
         copy.start()
-    lower, upper = pl.ds(0, 512), pl.ds(512, 512)
+    lower, upper = raw.at[ring(x, 3), 0:368], raw.at[ring(x, 1), 368:FEAT]
     tok_far = [
-        remote(tok.at[ring(x, 3), lower], tok.at[ring(x, 3), lower], tok_send.at[2], tok_recv.at[2], right),
-        remote(tok.at[ring(x, 1), upper], tok.at[ring(x, 1), upper], tok_send.at[3], tok_recv.at[3], left),
+        remote(lower, lower, tok_send.at[2], tok_recv.at[2], right),
+        remote(upper, upper, tok_send.at[3], tok_recv.at[3], left),
     ]
 
-    def encode(slot, ab, to):
-        @pl.loop(0, 3, unroll=3)
+    def encode(slot, ab, e, to):
+        @pl.loop(0, 6, unroll=3)
         def _(j):
             rows = pl.ds(pl.multiple_of(j * TILE, TILE), TILE)
             for lane in range(COLS // LANES):
                 cols = slice(lane * LANES, (lane + 1) * LANES)
                 block = stage[slot, ab, rows, :, cols].reshape(BLOCK, LANES)
-                for zz in range(RING):
-                    weight = jnp.dot(swap[zz * 64 : zz * 64 + 64, :], block, preferred_element_type=F32)
-                    ob[*to, zz, :, :, rows, cols] = restore(weight, groups[...]).reshape(2, 2, TILE, LANES)
+                for n in (0, 1):
+                    weight = jnp.dot(swap[e, n * 64 : n * 64 + 64, :], block, preferred_element_type=F32)
+                    ob[*to, 2 * n : 2 * n + 2, :, rows, cols] = restore(weight, groups[...]).reshape(2, 2, TILE, LANES)
 
     def first_y(q, step):
         to = ring(y, step)
@@ -186,15 +165,15 @@
     @pl.loop(0, 8)
     def _(n):
         slot, q, i = n % 2, n // 4, n % 4
-        load_wait(gate_w, q, ring(y, i + 1), slot, 0)
-        load_wait(up_w, q, i, slot, 1)
+        load(gate_w, ring(y, i + 1), slot, 0).wait()
+        load(up_w, i, slot, 1).wait()
 
         @pl.when(n < 7)
         def _():
-            load_start(gate_w, (n + 1) // 4, ring(y, n + 2), 1 - slot, 0)
-            load_start(up_w, (n + 1) // 4, (n + 1) % 4, 1 - slot, 1)
-
-        encode(slot, 0, (0, q, ring(y, i + 1)))
+            load(gate_w, ring(y, n + 2), 1 - slot, 0).start()
+            load(up_w, (n + 1) % 4, 1 - slot, 1).start()
+
+        encode(slot, 0, q, (0, q, ring(y, i + 1)))
 
         @pl.when(i == 3)
         def _():
@@ -205,24 +184,23 @@
         def _():
             remote(*first_y(q, i + 1)).start()
 
-        encode(slot, 1, (1, q, i))
+        encode(slot, 1, q, (1, q, i))
         for step in (2, 1, 3):
             remote(*first_z(q, step, i)).start()
         src, dst, _, recv, _ = first_z(q, 0, i)
         pltpu.make_async_copy(src, dst, recv).start()
 
-    load_start(down_w, 0, 0, 0, 0)
+    load(down_w, 0, 0, 0).start()
     everything = slice(None)
 
     def second(q):
         local, far = [], []
-        rows = pl.ds(q * 48, 48)
         for step in (2, 1, 3, 0):
             for dc in (0, 1):
                 cc = (c + dc) % 2
                 zz, yy = ring(z, step), ring(y, step)
-                a = (mid.at[0, q, :, zz, cc], inbox.at[0:4, z, c, :, rows])
-                b = (mid.at[1, q, :, yy, cc], inbox.at[4 + y, :, c, :, rows])
+                a = (mid.at[0, q, :, zz, cc], inbox.at[0:4, z, c, q])
+                b = (mid.at[1, q, :, yy, cc], inbox.at[4 + y, :, c, q])
                 if step == 0 and dc == 0:
                     local += [pltpu.make_async_copy(*pair, s2_recv.at[ab, q, 0, 0]) for ab, pair in enumerate((a, b))]
                     continue
@@ -251,22 +229,23 @@
 
     sent(0)
 
-    @pl.loop(0, 8)
+    @pl.loop(0, 4)
     def _(n):
-        slot, h, yy = n % 2, n // 4, n % 4
-        load_wait(down_w, h, yy, slot, 0)
-
-        @pl.when(n < 7)
+        slot = n % 2
+        load(down_w, n, slot, 0).wait()
+
+        @pl.when(n < 3)
         def _():
-            load_start(down_w, (n + 1) // 4, (n + 1) % 4, 1 - slot, 0)
-
-        encode(slot, 0, (h, 0, yy))
+            load(down_w, n + 1, 1 - slot, 0).start()
+
+        for e in (0, 1):
+            encode(slot, 0, e, (e, 0, n))
 
     shuffles = []
     for cc in (0, 1):
         for h in (0, 1):
             to = 2 * c + h
-            src, dst = ob.at[h, 0, :, :, cc], xs.at[x]
+            src, dst = ob.at[:, 0, :, :, cc, 48 * h : 48 * h + 48], xs.at[x]
             own = jnp.logical_and(cc == c, to == x)
             far = remote(src, dst, xs_send.at[cc, h], xs_recv.at[x], device(y, z, cc, to))
             near = pltpu.make_async_copy(src, dst, xs_recv.at[x])
@@ -283,28 +262,53 @@
         for copy in far:
             copy.wait_recv()
 
-    def products(q):
-        @pl.loop(0, 8)
+    def show(n):
+        return pltpu.make_async_copy(raw.at[ring(x, n)], shown.at[n % 2], shown_sem.at[n % 2])
+
+    for copy in tok_far:
+        copy.wait_recv()
+    own_tokens = pltpu.make_async_copy(tokens, shown.at[0], shown_sem.at[0])
+    own_tokens.start()
+    for n in range(RING):
+        if n < RING - 1:
+            show(n + 1).start()
+        (show(n) if n else own_tokens).wait()
+
+        @pl.loop(0, 4)
+        def _(i):
+            rows = pl.ds(pl.multiple_of(i * 256, 256), 256)
+            tok[ring(x, n), rows, :] = lax.dot_general(
+                shown[n % 2, :, rows], place[...], (((0,), (0,)), ((), ())), preferred_element_type=F32
+            ).astype(BF16)
+
+    def products(e):
+        @pl.loop(0, 4)
         def _(n):
-            e, rows = n // 4, pl.ds(pl.multiple_of(n % 4 * 256, 256), 256)
+            rows = pl.ds(pl.multiple_of(n * 256, 256), 256)
             made = []
             for ab in (0, 1):
-                total = None if q == 0 else sums[e, ab, rows, :]
+                total = None
                 for s in range(RING):
-                    weight = inbox[4 * ab + s, :, :, e, q * 48 : q * 48 + 48].reshape(WIDE // 2, COLS)
-                    picked = tok[s, rows, q * (WIDE // 2) : (q + 1) * (WIDE // 2)]
-                    part = jnp.dot(picked, weight, preferred_element_type=F32)
+                    weight = inbox[4 * ab + s, :, :, e].reshape(WIDE, COLS)
+                    part = jnp.dot(tok[s, rows, :], weight, preferred_element_type=F32)
                     total = part if total is None else total + part
                 made.append(total)
-            if q == 0:
-                sums[e, 0, rows, :], sums[e, 1, rows, :] = made
-            else:
-                gate, up = made
-                hid2[e, rows, :] = ((up + 1.0) * gate * jax.nn.sigmoid(1.702 * gate)).astype(BF16)
+            gate, up = made
+            hid[x, e, rows, :] = ((up + 1.0) * gate * jax.nn.sigmoid(1.702 * gate)).astype(BF16)
+
+    hid_near, hid_far = [], []
+    for h in (0, 1):
+        own, below, above = hid.at[x, h], hid.at[ring(x, 3), h, 0:512], hid.at[ring(x, 1), h, 512:TOK]
+        hid_near.append([
+            remote(own, own, hid_send.at[h, 0], hid_recv.at[h, 0], right),
+            remote(own, own, hid_send.at[h, 1], hid_recv.at[h, 1], left),
+        ])
+        hid_far.append([
+            remote(below, below, hid_send.at[h, 2], hid_recv.at[h, 2], right),
+            remote(above, above, hid_send.at[h, 3], hid_recv.at[h, 3], left),
+        ])
 
     arrived(second_0)
-    for copy in tok_far:
-        copy.wait_recv()
     products(0)
 
     for n in range(RING):
@@ -315,8 +319,8 @@
         for step in (2, 1, 3, 0):
             yy, zz = ring(y, step), ring(z, step)
             rows = pl.ds(r * TILE, TILE)
-            a = (xs.at[:, yy, :, 0, rows], midd.at[0, r, :, y])
-            b = (xs.at[:, :, zz, 1, rows], midd.at[1, r, :, z])
+            a = (xs.at[:, 0, yy, :, rows], midd.at[0, r, :, y])
+            b = (xs.at[:, 1, :, zz, rows], midd.at[1, r, :, z])
             if step == 0:
                 local += [pltpu.make_async_copy(*pair, d1_recv.at[ab, r, 0]) for ab, pair in enumerate((a, b))]
                 continue
@@ -345,35 +349,16 @@
     down_2 = [down_second(r) for r in range(CHUNKS)]
     for copies in down_1:
         start(copies)
+    for copy in hid_near[0]:
+        copy.start()
 
     arrived(second_1)
     products(1)
+    for copy in hid_near[1]:
+        copy.start()
 
     load_order = pltpu.make_async_copy(order, inbox, order_sem)
     load_order.start()
-
-    first, total = counts[0], counts[0] + counts[1]
-    lanes = lax.broadcasted_iota(jnp.int32, (BLOCK, TOK), 1)
-    hid_near, hid_far = [], []
-    for h in (0, 1):
-        for n in range(RING):
-            slot = 2 * n + h
-            row = jnp.where(slot < total, picks[:, slot : slot + 1], -1)
-            pick = (row == lanes).astype(F32).astype(BF16)
-            which = (slot >= first).astype(jnp.int32)
-            hid[x, h, n] = jnp.dot(pick, hid2[which], preferred_element_type=F32).astype(BF16)
-
-        own, below, above = hid.at[x, h], hid.at[ring(x, 3), h, pl.ds(0, 2)], hid.at[ring(x, 1), h, pl.ds(2, 2)]
-        hid_near.append([
-            remote(own, own, hid_send.at[h, 0], hid_recv.at[h, 0], right),
-            remote(own, own, hid_send.at[h, 1], hid_recv.at[h, 1], left),
-        ])
-        hid_far.append([
-            remote(below, below, hid_send.at[h, 2], hid_recv.at[h, 2], right),
-            remote(above, above, hid_send.at[h, 3], hid_recv.at[h, 3], left),
-        ])
-        for copy in hid_near[h]:
-            copy.start()
 
     def hid_forward(h):
         for near, far in zip(hid_near[h], hid_far[h]):
@@ -391,43 +376,56 @@
 
     results = []
 
-    def project(h, r):
-        for step in (2, 1, 3, 0):
-            to = ring(x, step)
-            which = (2 * to + h >= first).astype(jnp.int32)
-            made = None
-            for s in range(RING):
-                part = lax.dot_general(
-                    hid[s, h, to],
-                    in_d[r][which, s].reshape(BLOCK, COLS),
-                    (((1,), (1,)), ((), ())),
-                    preferred_element_type=F32,
-                )
-                made = part if made is None else made + part
-            if step == 0:
-                fin[x, h, r] = made.astype(BF16)
-                continue
-            ob_out[step - 1, h, r] = made.astype(BF16)
-            copy = remote(
-                ob_out.at[step - 1, h, r], fin.at[x, h, r], out_send.at[h, r, step - 1], out_recv.at[h, r, step - 1],
-                device(y, z, c, to),
+    first, total = counts[0], counts[0] + counts[1]
+    lanes = lax.broadcasted_iota(jnp.int32, (BLOCK, LANES), 1)
+
+    def pick(h, step):
+        slot = 2 * ring(x, step) + h
+        row = jnp.where(slot < total, picks[slot], -1)
+        chosen = jnp.concatenate([(row - n * LANES == lanes).astype(F32) for n in range(TOK // LANES)], axis=1).astype(BF16)
+        which = (slot >= first).astype(jnp.int32)
+        for s in range(RING):
+            picked[step, s] = jnp.dot(chosen, hid[s, which], preferred_element_type=F32).astype(BF16)
+
+    def project(h, r, step):
+        to = ring(x, step)
+        which = (2 * to + h >= first).astype(jnp.int32)
+        made = None
+        for s in range(RING):
+            part = lax.dot_general(
+                picked[step, s],
+                in_d[r][which, s].reshape(BLOCK, COLS),
+                (((1,), (1,)), ((), ())),
+                preferred_element_type=F32,
             )
-            copy.start()
-            results.append((h, r, copy))
-
-    for copy in hid_far[0]:
+            made = part if made is None else made + part
+        if step == 0:
+            fin[x, h, r] = made.astype(BF16)
+            return
+        ob_out[step - 1, h, r] = made.astype(BF16)
+        copy = remote(
+            ob_out.at[step - 1, h, r], fin.at[x, h, r], out_send.at[h, r, step - 1], out_recv.at[h, r, step - 1],
+            device(y, z, c, to),
+        )
+        copy.start()
+        results.append((h, r, copy))
+
+    for copy in hid_far[0] + hid_far[1]:
         copy.wait_recv()
     arrived(down_2[0])
-    project(0, 0)
+    for step in (2, 1, 3, 0):
+        pick(0, step)
+        project(0, 0, step)
     arrived(down_2[1])
-    project(0, 1)
-    for copy in hid_far[1]:
-        copy.wait_recv()
-    project(1, 0)
-    project(1, 1)
+    for step in (2, 1, 3, 0):
+        project(0, 1, step)
     arrived(down_2[2])
-    project(0, 2)
-    project(1, 2)
+    for step in (2, 1, 3, 0):
+        project(0, 2, step)
+    for step in (2, 1, 3, 0):
+        pick(1, step)
+        for r in range(CHUNKS):
+            project(1, r, step)
 
     load_order.wait()
 
@@ -480,26 +478,28 @@
         kernel,
         out_shape=(
             jax.ShapeDtypeStruct((D, 2 * BLOCK), BF16),
-            jax.ShapeDtypeStruct((2, 2, RING, RING, 2, 2, 48, COLS), BF16),
-            jax.ShapeDtypeStruct((RING, RING, RING, 2, 48, COLS), BF16),
+            jax.ShapeDtypeStruct((2, 2, RING, RING, 2, PAD, COLS), BF16),
+            jax.ShapeDtypeStruct((RING, 2, RING, RING, 48, COLS), BF16),
             jax.ShapeDtypeStruct((2, CHUNKS, RING, RING, RING, TILE, COLS), BF16),
+            jax.ShapeDtypeStruct((RING, FEAT, TOK), BF16),
         ),
-        in_specs=[vmem, hbm, hbm, hbm, vmem, pl.BlockSpec(memory_space=pltpu.SMEM), vmem, vmem, vmem, hbm],
-        out_specs=(vmem, hbm, hbm, hbm),
+        in_specs=[hbm, hbm, hbm, hbm, vmem, pl.BlockSpec(memory_space=pltpu.SMEM), vmem, vmem, vmem, hbm],
+        out_specs=(vmem, hbm, hbm, hbm, hbm),
         scratch_shapes=[
-            pltpu.VMEM((2, 2, RING, RING, 2, 2, 48, COLS), BF16),
+            pltpu.VMEM((2, 2, RING, RING, 2, PAD, COLS), BF16),
             pltpu.VMEM((9, RING, 2, 2, PAD, COLS), BF16),
             pltpu.VMEM((RING, TOK, WIDE), BF16),
-            pltpu.VMEM((2, 2, 48, 16, COLS), BF16),
+            pltpu.VMEM((2, 2, PAD, 16, COLS), BF16),
             *[pltpu.VMEM((2, RING, RING, RING, TILE, COLS), BF16) for _ in range(CHUNKS)],
-            pltpu.VMEM((2, TOK, COLS), BF16),
-            pltpu.VMEM((RING, 2, RING, BLOCK, COLS), BF16),
+            pltpu.VMEM((RING, 2, TOK, COLS), BF16),
+            pltpu.VMEM((RING, RING, BLOCK, COLS), BF16),
             pltpu.VMEM((3, 2, CHUNKS, BLOCK, BLOCK), BF16),
             pltpu.VMEM((RING, 2, CHUNKS, BLOCK, BLOCK), BF16),
-            pltpu.VMEM((BLOCK, SLOTS), jnp.int32),
-            pltpu.VMEM((2, 2, TOK, COLS), F32),
-            dma((2, 2, 2)),
+            pltpu.VMEM((SLOTS, BLOCK, LANES), jnp.int32),
+            pltpu.VMEM((2, FEAT, TOK), BF16),
+            dma((2, 2)),
             dma,
+            dma((2,)),
             dma((2, 2, RING)), dma((2, 2, RING)),
             dma((2, 2, RING, 2)), dma((2, 2, RING, 2)),
             dma((2, 2)), dma((RING,)),

time: 226 us -> 212 us (0.938)
  Pallas kernels: 223 us -> 208 us
    pallas_call x1, Pallas kernels: 223 us -> 208 us  [body(): pl.pallas_call(kernel, out_shape=(jax.ShapeDtypeStruct((D, 2 * BLOCK), BF...]
where the time goes in v3:
time: 212 us
  Pallas kernels  208 us (98%)
  local copies, waits for them, and re-layouts  3.62 us (2%)
    pallas_call x1, Pallas kernels, body(): pl.pallas_call(kernel, out_shape=(jax.ShapeDtypeStruct((D, 2 * BLOCK), BF...  208 us

profile of v3, /device:TPU:1, one launch (start us, length us, event | category | flops | bytes accessed | tf_op | source)
XLA Modules:
  0.0 211.5 jit_solution(2243859925222461988)
XLA Ops:
  0.0 207.9 %shard_map.100 = (bf16[2880,512]{1,0:T(8,128)(2,1)}, bf16[2,2,4,4,2,96,384]{6,5,4,3,2,1,0:T(8,128)(2,1)}, bf16[4,2,4,4,48,384]{5,4,3,2,1,0:T(8,128)(2,1)}, bf16[...) custom-call(bf16[720,1024]{1,0:T(8,128)(2,1)} %bitcast.9, bf16[90,64,384]{2,1,0:T(8,128)(2,1)} %bitcast.5, ...), custom_call_target="tpu_custom_call" | custom-call | tf_op jit(solution)/shard_map/pallas_call | solution.py:477
  207.9 3.6 %copy.12 = bf16[512,2880]{0,1:T(8,128)(2,1)} copy(bf16[512,2880]{0,1:T(8,128)(2,1)} %bitcast.8) | data formatting | bytes 5898240

commit v4 on v3

--- a/solution.py
+++ b/solution.py
@@ -85,11 +85,12 @@
 def kernel(
     tokens, gate_w, up_w, down_w, block_tokens, counts, place, groups, swap, order,
     out, mid, xs, midd, raw,
-    ob, inbox, tok, stage, in_0, in_1, in_2, hid, picked, ob_out, fin, picks, shown,
-    stage_sem, order_sem, shown_sem, s1_send, s1_recv, s2_send, s2_recv, xs_send, xs_recv,
+    ob, inbox, tok, stage, in_0, in_1, in_2, hid_0, hid_1, hid_2, hid_3, ob_out, fin, picks, shown, made_out,
+    stage_sem, order_sem, shown_sem, made_sem, s1_send, s1_recv, s2_send, s2_recv, xs_send, xs_recv,
     d1_send, d1_recv, d2_send, d2_recv, tok_send, tok_recv, hid_send, hid_recv, out_send, out_recv,
 ):
     in_d = (in_0, in_1, in_2)
+    hid = (hid_0, hid_1, hid_2, hid_3)
     me, x = lax.axis_index("expert"), lax.axis_index("shard")
     y, z, c = me // 8, (me // 2) % 4, me % 2
 
@@ -227,6 +228,13 @@
         near.wait_recv()
         far.start()
 
+    def shuffle(cc, h, yy):
+        to = 2 * c + h
+        src, dst = ob.at[:, 0, yy, :, cc, 48 * h : 48 * h + 48], xs.at[x, :, yy]
+        far = remote(src, dst, xs_send.at[cc, h], xs_recv.at[x], device(y, z, cc, to))
+        near = pltpu.make_async_copy(src, dst, xs_recv.at[x])
+        return jnp.logical_and(cc == c, to == x), near, far
+
     sent(0)
 
     @pl.loop(0, 4)
@@ -240,18 +248,11 @@
 
         for e in (0, 1):
             encode(slot, 0, e, (e, 0, n))
-
-    shuffles = []
-    for cc in (0, 1):
-        for h in (0, 1):
-            to = 2 * c + h
-            src, dst = ob.at[:, 0, :, :, cc, 48 * h : 48 * h + 48], xs.at[x]
-            own = jnp.logical_and(cc == c, to == x)
-            far = remote(src, dst, xs_send.at[cc, h], xs_recv.at[x], device(y, z, cc, to))
-            near = pltpu.make_async_copy(src, dst, xs_recv.at[x])
-            pl.when(own)(near.start)
-            pl.when(jnp.logical_not(own))(far.start)
-            shuffles.append((own, far))
+        for cc in (0, 1):
+            for h in (0, 1):
+                own, near, far = shuffle(cc, h, n)
+                pl.when(own)(near.start)
+                pl.when(jnp.logical_not(own))(far.start)
 
     second_1 = pass_on(1)
 
@@ -294,22 +295,24 @@
                     total = part if total is None else total + part
                 made.append(total)
             gate, up = made
-            hid[x, e, rows, :] = ((up + 1.0) * gate * jax.nn.sigmoid(1.702 * gate)).astype(BF16)
+            hid_0[e, rows, :] = ((up + 1.0) * gate * jax.nn.sigmoid(1.702 * gate)).astype(BF16)
 
     hid_near, hid_far = [], []
-    for h in (0, 1):
-        own, below, above = hid.at[x, h], hid.at[ring(x, 3), h, 0:512], hid.at[ring(x, 1), h, 512:TOK]
+    low, high = slice(0, 512), slice(512, TOK)
+    for e in (0, 1):
         hid_near.append([
-            remote(own, own, hid_send.at[h, 0], hid_recv.at[h, 0], right),
-            remote(own, own, hid_send.at[h, 1], hid_recv.at[h, 1], left),
+            remote(hid_0.at[e], hid_1.at[e], hid_send.at[e, 0], hid_recv.at[e, 0], right),
+            remote(hid_0.at[e], hid_2.at[e], hid_send.at[e, 1], hid_recv.at[e, 1], left),
         ])
         hid_far.append([
-            remote(below, below, hid_send.at[h, 2], hid_recv.at[h, 2], right),
-            remote(above, above, hid_send.at[h, 3], hid_recv.at[h, 3], left),
+            remote(hid_1.at[e, low], hid_3.at[e, low], hid_send.at[e, 2], hid_recv.at[e, 2], right),
+            remote(hid_2.at[e, high], hid_3.at[e, high], hid_send.at[e, 3], hid_recv.at[e, 3], left),
         ])
 
     arrived(second_0)
     products(0)
+    for copy in hid_near[0]:
+        copy.start()
 
     for n in range(RING):
         landed(xs.at[n], xs_recv.at[n])
@@ -349,8 +352,6 @@
     down_2 = [down_second(r) for r in range(CHUNKS)]
     for copies in down_1:
         start(copies)
-    for copy in hid_near[0]:
-        copy.start()
 
     arrived(second_1)
     products(1)
@@ -379,22 +380,25 @@
     first, total = counts[0], counts[0] + counts[1]
     lanes = lax.broadcasted_iota(jnp.int32, (BLOCK, LANES), 1)
 
-    def pick(h, step):
+    def kept(h, step, n):
+        return step, slice(n * BLOCK, (n + 1) * BLOCK), slice(h * COLS, (h + 1) * COLS)
+
+    def pick(h, step, shards):
         slot = 2 * ring(x, step) + h
         row = jnp.where(slot < total, picks[slot], -1)
         chosen = jnp.concatenate([(row - n * LANES == lanes).astype(F32) for n in range(TOK // LANES)], axis=1).astype(BF16)
         which = (slot >= first).astype(jnp.int32)
-        for s in range(RING):
-            picked[step, s] = jnp.dot(chosen, hid[s, which], preferred_element_type=F32).astype(BF16)
+        for n in shards:
+            tok[kept(h, step, n)] = jnp.dot(chosen, hid[n][which], preferred_element_type=F32).astype(BF16)
 
     def project(h, r, step):
         to = ring(x, step)
         which = (2 * to + h >= first).astype(jnp.int32)
         made = None
-        for s in range(RING):
+        for n, away in enumerate((0, 3, 1, 2)):
             part = lax.dot_general(
-                picked[step, s],
-                in_d[r][which, s].reshape(BLOCK, COLS),
+                tok[kept(h, step, n)],
+                in_d[r][which, ring(x, away)].reshape(BLOCK, COLS),
                 (((1,), (1,)), ((), ())),
                 preferred_element_type=F32,
             )
@@ -410,22 +414,25 @@
         copy.start()
         results.append((h, r, copy))
 
+    for step in (2, 1, 3, 0):
+        pick(0, step, (0, 1, 2))
+    arrived(down_2[0])
     for copy in hid_far[0] + hid_far[1]:
         copy.wait_recv()
-    arrived(down_2[0])
     for step in (2, 1, 3, 0):
-        pick(0, step)
+        pick(0, step, (3,))
         project(0, 0, step)
     arrived(down_2[1])
     for step in (2, 1, 3, 0):
         project(0, 1, step)
+    for step in (2, 1, 3, 0):
+        pick(1, step, (0, 1, 2, 3))
+        project(1, 0, step)
+        project(1, 1, step)
     arrived(down_2[2])
-    for step in (2, 1, 3, 0):
-        project(0, 2, step)
-    for step in (2, 1, 3, 0):
-        pick(1, step)
-        for r in range(CHUNKS):
-            project(1, r, step)
+    for h in (0, 1):
+        for step in (2, 1, 3, 0):
+            project(h, 2, step)
 
     load_order.wait()
 
@@ -443,30 +450,44 @@
             result = part if result is None else result + part
         return result
 
+    def keep(b, h):
+        rows = pl.ds(pl.multiple_of(b * OUTB, OUTB), OUTB) if not isinstance(b, int) else pl.ds(b * OUTB, min(OUTB, D - b * OUTB))
+        spot = (rows, slice(h * BLOCK, (h + 1) * BLOCK))
+        return spot, pltpu.make_async_copy(made_out.at[spot], out.at[spot], made_sem.at[h, b])
+
+    def store(b, h, value):
+        spot, copy = keep(b, h)
+        made_out[spot] = value.astype(BF16)
+        copy.start()
+
     for h in (0, 1):
         for hh, _, copy in results:
             if hh == h:
                 copy.wait_recv()
-        rows = slice(h * BLOCK, (h + 1) * BLOCK)
 
         @pl.loop(0, 3)
         def _(b):
-            out[pl.ds(pl.multiple_of(b * OUTB, OUTB), OUTB), rows] = ordered(h, 0, b).astype(BF16)
-
-        out[3 * OUTB : 4 * OUTB, rows] = (ordered(h, 0, 3) + ordered(h, 1, 8)).astype(BF16)
+            store(b, h, ordered(h, 0, b))
+
+        store(3, h, ordered(h, 0, 3) + ordered(h, 1, 8))
 
         @pl.loop(4, 7)
         def _(b):
-            out[pl.ds(pl.multiple_of(b * OUTB, OUTB), OUTB), rows] = ordered(h, 1, b).astype(BF16)
-
-        out[7 * OUTB : D, rows] = ordered(h, 1, 7)[: D - 7 * OUTB].astype(BF16)
+            store(b, h, ordered(h, 1, b))
+
+        store(7, h, ordered(h, 1, 7)[: D - 7 * OUTB])
 
     sent(1)
-    for own, far in shuffles:
-        pl.when(jnp.logical_not(own))(far.wait_send)
+    for cc in (0, 1):
+        for h in (0, 1):
+            own, _, far = shuffle(cc, h, everything)
+            pl.when(jnp.logical_not(own))(far.wait_send)
     for copies in (second_0, second_1, *down_1, *down_2):
         for copy in copies[1]:
             copy.wait_send()
+    for h in (0, 1):
+        for b in range(8):
+            keep(b, h)[1].wait()
     for copy in tok_near + tok_far + sum(hid_near + hid_far, []) + [copy for _, _, copy in results]:
         copy.wait_send()
 
@@ -484,22 +505,23 @@
             jax.ShapeDtypeStruct((RING, FEAT, TOK), BF16),
         ),
         in_specs=[hbm, hbm, hbm, hbm, vmem, pl.BlockSpec(memory_space=pltpu.SMEM), vmem, vmem, vmem, hbm],
-        out_specs=(vmem, hbm, hbm, hbm, hbm),
+        out_specs=(hbm, hbm, hbm, hbm, hbm),
         scratch_shapes=[
             pltpu.VMEM((2, 2, RING, RING, 2, PAD, COLS), BF16),
             pltpu.VMEM((9, RING, 2, 2, PAD, COLS), BF16),
             pltpu.VMEM((RING, TOK, WIDE), BF16),
             pltpu.VMEM((2, 2, PAD, 16, COLS), BF16),
             *[pltpu.VMEM((2, RING, RING, RING, TILE, COLS), BF16) for _ in range(CHUNKS)],
-            pltpu.VMEM((RING, 2, TOK, COLS), BF16),
-            pltpu.VMEM((RING, RING, BLOCK, COLS), BF16),
+            *[pltpu.VMEM((2, TOK, COLS), BF16) for _ in range(RING)],
             pltpu.VMEM((3, 2, CHUNKS, BLOCK, BLOCK), BF16),
             pltpu.VMEM((RING, 2, CHUNKS, BLOCK, BLOCK), BF16),
             pltpu.VMEM((SLOTS, BLOCK, LANES), jnp.int32),
             pltpu.VMEM((2, FEAT, TOK), BF16),
+            pltpu.VMEM((D, 2 * BLOCK), BF16),
             dma((2, 2)),
             dma,
             dma((2,)),
+            dma((2, 8)),
             dma((2, 2, RING)), dma((2, 2, RING)),
             dma((2, 2, RING, 2)), dma((2, 2, RING, 2)),
             dma((2, 2)), dma((RING,)),

time: 212 us -> 210 us (level)
    pallas_call x1, Pallas kernels: 208 us -> 206 us  [body(): pl.pallas_call(kernel, out_shape=(jax.ShapeDtypeStruct((D, 2 * BLOCK), BF...]
where the time goes in v4:
time: 210 us; the launch traced here: 209 us
  Pallas kernels  206 us (98%)
  local copies, waits for them, and re-layouts  3.62 us (2%)
    pallas_call x1, Pallas kernels, body(): pl.pallas_call(kernel, out_shape=(jax.ShapeDtypeStruct((D, 2 * BLOCK), BF...  206 us

profile of v4, /device:TPU:1, one launch (start us, length us, event | category | flops | bytes accessed | tf_op | source)
XLA Modules:
  0.0 209.2 jit_solution(12475979892057064396)
XLA Ops:
  0.0 205.6 %shard_map.100 = (bf16[2880,512]{1,0:T(8,128)(2,1)}, bf16[2,2,4,4,2,96,384]{6,5,4,3,2,1,0:T(8,128)(2,1)}, bf16[4,2,4,4,48,384]{5,4,3,2,1,0:T(8,128)(2,1)}, bf16[...) custom-call(bf16[720,1024]{1,0:T(8,128)(2,1)} %bitcast.9, bf16[90,64,384]{2,1,0:T(8,128)(2,1)} %bitcast.5, ...), custom_call_target="tpu_custom_call" | custom-call | tf_op jit(solution)/shard_map/pallas_call | solution.py:498
  205.6 3.6 %copy.12 = bf16[512,2880]{0,1:T(8,128)(2,1)} copy(bf16[512,2880]{0,1:T(8,128)(2,1)} %bitcast.8) | data formatting | bytes 5898240

commit v5 on v4

--- a/solution.py
+++ b/solution.py
@@ -123,11 +123,6 @@
 
     load(gate_w, ring(y, 1), 0, 0).start()
     load(up_w, 0, 0, 1).start()
-    stage[:, :, ROWS:PAD] = jnp.zeros((2, 2, PAD - ROWS, 16, COLS), BF16)
-    turned = jnp.transpose(block_tokens[...])
-    for n in range(SLOTS):
-        picks[n] = jnp.broadcast_to(turned[:, n : n + 1], (BLOCK, LANES))
-
     pl.semaphore_wait(barrier, len(peers))
 
     right, left = device(y, z, c, ring(x, 1)), device(y, z, c, ring(x, 3))
@@ -142,6 +137,8 @@
         remote(lower, lower, tok_send.at[2], tok_recv.at[2], right),
         remote(upper, upper, tok_send.at[3], tok_recv.at[3], left),
     ]
+
+    stage[:, :, ROWS:PAD] = jnp.zeros((2, 2, PAD - ROWS, 16, COLS), BF16)
 
     def encode(slot, ab, e, to):
         @pl.loop(0, 6, unroll=3)
@@ -263,6 +260,10 @@
         for copy in far:
             copy.wait_recv()
 
+    turned = jnp.transpose(block_tokens[...])
+    for n in range(SLOTS):
+        picks[n] = jnp.broadcast_to(turned[:, n : n + 1], (BLOCK, LANES))
+
     def show(n):
         return pltpu.make_async_copy(raw.at[ring(x, n)], shown.at[n % 2], shown_sem.at[n % 2])
 
@@ -282,8 +283,8 @@
                 shown[n % 2, :, rows], place[...], (((0,), (0,)), ((), ())), preferred_element_type=F32
             ).astype(BF16)
 
-    def products(e):
-        @pl.loop(0, 4)
+    def products(e, half):
+        @pl.loop(2 * half, 2 * half + 2)
         def _(n):
             rows = pl.ds(pl.multiple_of(n * 256, 256), 256)
             made = []
@@ -301,18 +302,29 @@
     low, high = slice(0, 512), slice(512, TOK)
     for e in (0, 1):
         hid_near.append([
-            remote(hid_0.at[e], hid_1.at[e], hid_send.at[e, 0], hid_recv.at[e, 0], right),
-            remote(hid_0.at[e], hid_2.at[e], hid_send.at[e, 1], hid_recv.at[e, 1], left),
+            remote(hid_0.at[e, low], hid_1.at[e, low], hid_send.at[e, 0], hid_recv.at[e, 0], right),
+            remote(hid_0.at[e, high], hid_2.at[e, high], hid_send.at[e, 1], hid_recv.at[e, 1], left),
+            remote(hid_0.at[e, high], hid_1.at[e, high], hid_send.at[e, 2], hid_recv.at[e, 2], right),
+            remote(hid_0.at[e, low], hid_2.at[e, low], hid_send.at[e, 3], hid_recv.at[e, 3], left),
         ])
         hid_far.append([
-            remote(hid_1.at[e, low], hid_3.at[e, low], hid_send.at[e, 2], hid_recv.at[e, 2], right),
-            remote(hid_2.at[e, high], hid_3.at[e, high], hid_send.at[e, 3], hid_recv.at[e, 3], left),
+            remote(hid_1.at[e, low], hid_3.at[e, low], hid_send.at[e, 4], hid_recv.at[e, 4], right),
+            remote(hid_2.at[e, high], hid_3.at[e, high], hid_send.at[e, 5], hid_recv.at[e, 5], left),
         ])
 
+    def gather_hidden(e):
+        products(e, 0)
+        hid_near[e][0].start()
+        products(e, 1)
+        for copy in hid_near[e][1:]:
+            copy.start()
+
+    def hid_forward(e, side):
+        hid_near[e][side].wait_recv()
+        hid_far[e][side].start()
+
     arrived(second_0)
-    products(0)
-    for copy in hid_near[0]:
-        copy.start()
+    gather_hidden(0)
 
     for n in range(RING):
         landed(xs.at[n], xs_recv.at[n])
@@ -354,26 +366,23 @@
         start(copies)
 
     arrived(second_1)
-    products(1)
-    for copy in hid_near[1]:
-        copy.start()
+    gather_hidden(1)
 
     load_order = pltpu.make_async_copy(order, inbox, order_sem)
     load_order.start()
 
-    def hid_forward(h):
-        for near, far in zip(hid_near[h], hid_far[h]):
-            near.wait_recv()
-            far.start()
-
     arrived(down_1[0])
     start(down_2[0])
-    hid_forward(0)
+    hid_forward(0, 0)
+    hid_forward(0, 1)
+    hid_forward(1, 0)
     arrived(down_1[1])
     start(down_2[1])
-    hid_forward(1)
+    hid_forward(1, 1)
     arrived(down_1[2])
     start(down_2[2])
+    for copy in hid_near[0][2:] + hid_near[1][2:]:
+        copy.wait_recv()
 
     results = []
 
@@ -528,7 +537,7 @@
             dma((2, CHUNKS, RING)), dma((2, CHUNKS, RING)),
             dma((2, CHUNKS, RING)), dma((2, CHUNKS, RING)),
             dma((RING,)), dma((RING,)),
-            dma((2, RING)), dma((2, RING)),
+            dma((2, 6)), dma((2, 6)),
             dma((2, CHUNKS, 3)), dma((2, CHUNKS, 3)),
         ],
         compiler_params=pltpu.CompilerParams(

time: 210 us -> 210 us (level)
  no operation moved by 1% of the time
where the time goes in v5:
time: 210 us; the launch traced here: 209 us
  Pallas kernels  206 us (98%)
  local copies, waits for them, and re-layouts  3.62 us (2%)
    pallas_call x1, Pallas kernels, body(): pl.pallas_call(kernel, out_shape=(jax.ShapeDtypeStruct((D, 2 * BLOCK), BF...  206 us

profile of v5, /device:TPU:1, one launch (start us, length us, event | category | flops | bytes accessed | tf_op | source)
XLA Modules:
  0.0 209.3 jit_solution(4717999002918315116)
XLA Ops:
  0.0 205.6 %shard_map.100 = (bf16[2880,512]{1,0:T(8,128)(2,1)}, bf16[2,2,4,4,2,96,384]{6,5,4,3,2,1,0:T(8,128)(2,1)}, bf16[4,2,4,4,48,384]{5,4,3,2,1,0:T(8,128)(2,1)}, bf16[...) custom-call(bf16[720,1024]{1,0:T(8,128)(2,1)} %bitcast.9, bf16[90,64,384]{2,1,0:T(8,128)(2,1)} %bitcast.5, ...), custom_call_target="tpu_custom_call" | custom-call | tf_op jit(solution)/shard_map/pallas_call | solution.py:507
  205.6 3.6 %copy.12 = bf16[512,2880]{0,1:T(8,128)(2,1)} copy(bf16[512,2880]{0,1:T(8,128)(2,1)} %bitcast.8) | data formatting | bytes 5898240

commit v6 on v4

--- a/solution.py
+++ b/solution.py
@@ -436,18 +436,24 @@
 
     load_order.wait()
 
-    def ordered(h, half, matrix):
+    def ordered(h, half, matrix, last):
+        table = inbox[matrix].reshape(RING * OUTB, OUTB)
+
+        def pieces(n, r):
+            left = table[n * OUTB : (n + 1) * OUTB, r * LANES : (r + 1) * LANES]
+            return left, fin[n, h, r, :, half * LANES : (half + 1) * LANES]
+
         result = None
-        table = inbox[matrix].reshape(RING * OUTB, OUTB)
-        for n in range(RING):
-            got = [fin[n, h, r, :, half * LANES : (half + 1) * LANES] for r in range(CHUNKS)]
-            part = lax.dot_general(
-                table[n * OUTB : (n + 1) * OUTB],
-                jnp.concatenate(got, axis=1),
-                (((1,), (1,)), ((), ())),
-                preferred_element_type=F32,
-            )
-            result = part if result is None else result + part
+        for n in range(0, RING, 2):
+            for pair in [[(n, 2), (n + 1, 2)]] if last else [[(n, 0), (n, 1)], [(n + 1, 0), (n + 1, 1)]]:
+                left, right = zip(*[pieces(*at) for at in pair])
+                part = lax.dot_general(
+                    jnp.concatenate(left, axis=1),
+                    jnp.concatenate(right, axis=1),
+                    (((1,), (1,)), ((), ())),
+                    preferred_element_type=F32,
+                )
+                result = part if result is None else result + part
         return result
 
     def keep(b, h):
@@ -455,27 +461,31 @@
         spot = (rows, slice(h * BLOCK, (h + 1) * BLOCK))
         return spot, pltpu.make_async_copy(made_out.at[spot], out.at[spot], made_sem.at[h, b])
 
-    def store(b, h, value):
+    def store(b, h, value, last):
         spot, copy = keep(b, h)
-        made_out[spot] = value.astype(BF16)
-        copy.start()
-
-    for h in (0, 1):
-        for hh, _, copy in results:
-            if hh == h:
-                copy.wait_recv()
-
-        @pl.loop(0, 3)
-        def _(b):
-            store(b, h, ordered(h, 0, b))
-
-        store(3, h, ordered(h, 0, 3) + ordered(h, 1, 8))
-
-        @pl.loop(4, 7)
-        def _(b):
-            store(b, h, ordered(h, 1, b))
-
-        store(7, h, ordered(h, 1, 7)[: D - 7 * OUTB])
+        if last:
+            made_out[spot] = (made_out[spot].astype(F32) + value).astype(BF16)
+            copy.start()
+        else:
+            made_out[spot] = value.astype(BF16)
+
+    for last in (False, True):
+        for h in (0, 1):
+            for hh, r, copy in results:
+                if hh == h and (r == 2) == last:
+                    copy.wait_recv()
+
+            @pl.loop(0, 3)
+            def _(b):
+                store(b, h, ordered(h, 0, b, last), last)
+
+            store(3, h, ordered(h, 0, 3, last) + ordered(h, 1, 8, last), last)
+
+            @pl.loop(4, 7)
+            def _(b):
+                store(b, h, ordered(h, 1, b, last), last)
+
+            store(7, h, ordered(h, 1, 7, last)[: D - 7 * OUTB], last)
 
     sent(1)
     for cc in (0, 1):

time: 210 us -> 207 us (0.986)
  Pallas kernels: 206 us -> 203 us
    pallas_call x1, Pallas kernels: 206 us -> 203 us  [body(): pl.pallas_call(kernel, out_shape=(jax.ShapeDtypeStruct((D, 2 * BLOCK), BF...]
where the time goes in v6:
time: 207 us
  Pallas kernels  203 us (98%)
  local copies, waits for them, and re-layouts  3.62 us (2%)
    pallas_call x1, Pallas kernels, body(): pl.pallas_call(kernel, out_shape=(jax.ShapeDtypeStruct((D, 2 * BLOCK), BF...  203 us

profile of v6, /device:TPU:1, one launch (start us, length us, event | category | flops | bytes accessed | tf_op | source)
XLA Modules:
  0.0 206.6 jit_solution(5823634954436776019)
XLA Ops:
  0.0 203.0 %shard_map.100 = (bf16[2880,512]{1,0:T(8,128)(2,1)}, bf16[2,2,4,4,2,96,384]{6,5,4,3,2,1,0:T(8,128)(2,1)}, bf16[4,2,4,4,48,384]{5,4,3,2,1,0:T(8,128)(2,1)}, bf16[...) custom-call(bf16[720,1024]{1,0:T(8,128)(2,1)} %bitcast.9, bf16[90,64,384]{2,1,0:T(8,128)(2,1)} %bitcast.5, ...), custom_call_target="tpu_custom_call" | custom-call | tf_op jit(solution)/shard_map/pallas_call | solution.py:508
  203.0 3.6 %copy.12 = bf16[512,2880]{0,1:T(8,128)(2,1)} copy(bf16[512,2880]{0,1:T(8,128)(2,1)} %bitcast.8) | data formatting | bytes 5898240

commit v7 on v6

--- a/solution.py
+++ b/solution.py
@@ -469,37 +469,45 @@
         else:
             made_out[spot] = value.astype(BF16)
 
+    outgoing = {last: [copy for _, r, copy in results if (r == 2) == last] for last in (False, True)}
+
+    def settle():
+        sent(1)
+        for cc in (0, 1):
+            for h in (0, 1):
+                own, _, far = shuffle(cc, h, everything)
+                pl.when(jnp.logical_not(own))(far.wait_send)
+        for copies in (second_0, second_1, *down_1, *down_2):
+            for copy in copies[1]:
+                copy.wait_send()
+        for copy in tok_near + tok_far + sum(hid_near + hid_far, []) + outgoing[False]:
+            copy.wait_send()
+
     for last in (False, True):
+        if last:
+            settle()
         for h in (0, 1):
             for hh, r, copy in results:
                 if hh == h and (r == 2) == last:
                     copy.wait_recv()
 
-            @pl.loop(0, 3)
+            @pl.loop(0, 3, unroll=3)
             def _(b):
                 store(b, h, ordered(h, 0, b, last), last)
 
             store(3, h, ordered(h, 0, 3, last) + ordered(h, 1, 8, last), last)
 
-            @pl.loop(4, 7)
+            @pl.loop(4, 7, unroll=3)
             def _(b):
                 store(b, h, ordered(h, 1, b, last), last)
 
             store(7, h, ordered(h, 1, 7, last)[: D - 7 * OUTB], last)
 
-    sent(1)
-    for cc in (0, 1):
-        for h in (0, 1):
-            own, _, far = shuffle(cc, h, everything)
-            pl.when(jnp.logical_not(own))(far.wait_send)
-    for copies in (second_0, second_1, *down_1, *down_2):
-        for copy in copies[1]:
-            copy.wait_send()
+    for copy in outgoing[True]:
+        copy.wait_send()
     for h in (0, 1):
         for b in range(8):
             keep(b, h)[1].wait()
-    for copy in tok_near + tok_far + sum(hid_near + hid_far, []) + [copy for _, _, copy in results]:
-        copy.wait_send()
 
 
 def body(tokens, gate_weight, up_weight, down_weight, block_counts, block_tokens):

time: 207 us -> 206 us (level)
  no operation moved by 1% of the time
where the time goes in v7:
time: 206 us; the launch traced here: 205 us
  Pallas kernels  202 us (98%)
  local copies, waits for them, and re-layouts  3.62 us (2%)
    pallas_call x1, Pallas kernels, body(): pl.pallas_call(kernel, out_shape=(jax.ShapeDtypeStruct((D, 2 * BLOCK), BF...  202 us

profile of v7, /device:TPU:1, one launch (start us, length us, event | category | flops | bytes accessed | tf_op | source)
XLA Modules:
  0.0 205.3 jit_solution(16957732161561999505)
XLA Ops:
  0.0 201.7 %shard_map.100 = (bf16[2880,512]{1,0:T(8,128)(2,1)}, bf16[2,2,4,4,2,96,384]{6,5,4,3,2,1,0:T(8,128)(2,1)}, bf16[4,2,4,4,48,384]{5,4,3,2,1,0:T(8,128)(2,1)}, bf16[...) custom-call(bf16[720,1024]{1,0:T(8,128)(2,1)} %bitcast.9, bf16[90,64,384]{2,1,0:T(8,128)(2,1)} %bitcast.5, ...), custom_call_target="tpu_custom_call" | custom-call | tf_op jit(solution)/shard_map/pallas_call | solution.py:516
  201.7 3.6 %copy.12 = bf16[512,2880]{0,1:T(8,128)(2,1)} copy(bf16[512,2880]{0,1:T(8,128)(2,1)} %bitcast.8) | data formatting | bytes 5898240
